TPU v7x, 128 devices: a whole 4x4x4 slice. The times are simulated.
128 devices in a mesh: shard: 8 (over z, core), ctx: 2 (over x_hi), tp: 8 (over x_lo, y).
Axes of the slice: x: 4 (x_hi: 2, x_lo: 2; x = x_hi * 2 + x_lo), y: 4, z: 4, core: 2. Of those that a mesh axis runs over, the one named last changes fastest.
Arguments:
- tokens: bfloat16 [8, 736, 1152], P('shard', 'ctx'), may hold values from -6 to 6
- image_count: int32 [8], P('shard'), may hold values from 0 to 1, as said below
- ln_gain: bfloat16 [2, 1152], P(None, 'shard'), may hold values from 0.25 to 1.75
- vec_bias: bfloat16 [4, 1152], P(None, 'shard'), may hold values from -3 to 3
- w_qkv: bfloat16 [3, 1152, 1152], P(None, 'shard', 'tp')
- qv_bias: bfloat16 [2, 1152], P(None, 'tp'), may hold values from -3 to 3
- w_out: bfloat16 [1152, 1152], P('tp', 'shard'), may hold values from -1.5 to 1.5
- w_fc1: bfloat16 [1152, 4304], P('shard', 'tp'), may hold values from -0.1875 to 0.1875
- fc1_bias: bfloat16 [4304], P('tp'), may hold values from -3 to 3
- w_fc2: bfloat16 [4304, 1152], P('tp', 'shard'), may hold values from -0.09375 to 0.09375
- cotangent: bfloat16 [8, 736, 1152], P('shard', 'ctx'), may hold values from -6 to 6
Outputs:
- layer_out: bfloat16 [8, 736, 1152], P('shard', 'ctx')
- grad_tokens: float32 [8, 736, 1152], P('shard', 'ctx')
- grad_ln_gain: float32 [2, 1152], P(None, 'shard')
- grad_vec_bias: float32 [4, 1152], P(None, 'shard')
- grad_qkv: float32 [3, 1152, 1152], P(None, 'shard', 'tp')
- grad_qv_bias: float32 [2, 1152], P(None, 'tp')
- grad_out: float32 [1152, 1152], P('tp', 'shard')
- grad_fc1: float32 [1152, 4304], P('shard', 'tp')
- grad_fc1_bias: float32 [4304], P('tp')
- grad_fc2: float32 [4304, 1152], P('tp', 'shard')
Inputs may be any that keep to these rules, and one draw needn't show every extreme that they name: image_count[j] live images fill the first slots of index j of shard; some index holds 1 and some holds none.
All inputs are finite; a program needn't handle non-finite values.
Results may differ from a plain program's by a relative error of at most 0.009.
The roundings to bfloat16 on the way count: a program that leaves them out, or rounds other values in their place, can miss the bound.
Values may be sent and summed in bfloat16 or wider, within the bound.
A program may use at most 64 MiB of HBM per device.

v0:
```python
import math

import jax
import jax.numpy as jnp
from jax import lax
from jax.sharding import PartitionSpec as P

HD = 72
IMG_TOK = 729


EPS = 1e-06
GELU_C = math.sqrt(2.0 / math.pi)
GELU_A = 0.044715


def normalize(values_in, gain, shift):
    centre = jnp.mean(values_in, axis=-1, keepdims=True)
    centred = values_in - centre
    variance = jnp.mean(centred * centred, axis=-1, keepdims=True)
    inv_std = lax.rsqrt(variance + EPS)
    normed = centred * inv_std
    return (normed * gain + shift, normed, inv_std)


def norm_back(upstream, normed, inv_std, gain):
    scaled = upstream * gain
    return inv_std * (
        scaled
        - jnp.mean(scaled, axis=-1, keepdims=True)
        - normed * jnp.mean(scaled * normed, axis=-1, keepdims=True)
    )


def gelu_tanh(inputs):
    inner = GELU_C * (inputs + GELU_A * inputs * inputs * inputs)
    return 0.5 * inputs * (1.0 + jnp.tanh(inner))


def gelu_slope(inputs):
    tangent = jnp.tanh(GELU_C * (inputs + GELU_A * inputs * inputs * inputs))
    return 0.5 * (1.0 + tangent) + 0.5 * inputs * (1.0 - tangent * tangent) * GELU_C * (
        1.0 + 3.0 * GELU_A * inputs * inputs
    )


def matmul(left, right):
    return jnp.dot(left, right, preferred_element_type=jnp.float32)


def contract_rows(left, right):
    return lax.dot_general(
        left, right, (((0,), (0,)), ((), ())), preferred_element_type=jnp.float32
    )


def contract_cols(left, right):
    return lax.dot_general(
        left, right, (((1,), (1,)), ((), ())), preferred_element_type=jnp.float32
    )


def per_device(
    tokens, image_count, ln_gain, vec_bias, w_qkv, qv_bias, w_out, w_fc1, fc1_bias, w_fc2, cotangent
):
    slots, rows, width = tokens.shape
    count_rows = slots * rows
    channels = w_qkv.shape[2]
    heads_here = channels // HD
    score_scale = HD ** (-0.5)
    positions = lax.axis_index("ctx") * rows + jnp.arange(rows)
    live_slot = jnp.arange(slots) < image_count[0]
    row_mask = (
        (live_slot[:, None] & (positions < IMG_TOK)[None, :])
        .astype(jnp.float32)
        .reshape(count_rows, 1)
    )
    qkv_full, out_full, fc1_full, fc2_full, gains_full, biases_full = (
        lax.all_gather(w_qkv, "shard", axis=1, tiled=True),
        lax.all_gather(w_out, "shard", axis=1, tiled=True),
        lax.all_gather(w_fc1, "shard", axis=0, tiled=True),
        lax.all_gather(w_fc2, "shard", axis=1, tiled=True),
        lax.all_gather(ln_gain, "shard", axis=1, tiled=True),
        lax.all_gather(vec_bias, "shard", axis=1, tiled=True),
    )
    gains = gains_full.astype(jnp.float32)
    biases = biases_full.astype(jnp.float32)
    qv_shift = qv_bias.astype(jnp.float32)
    residual_in = tokens.reshape(count_rows, width).astype(jnp.float32)
    normed_a, normed_one, inv_one = normalize(residual_in, gains[0], biases[0])
    attn_in = normed_a.astype(jnp.bfloat16)
    projected = jnp.einsum("nd,kdc->knc", attn_in, qkv_full, preferred_element_type=jnp.float32)
    query = (projected[0] + qv_shift[0]).astype(jnp.bfloat16)
    keys_local = projected[1].astype(jnp.bfloat16).reshape(slots, rows, channels)
    values_local = (projected[2] + qv_shift[1]).astype(jnp.bfloat16).reshape(slots, rows, channels)
    keys_all, values_all = (
        lax.all_gather(keys_local, "ctx", axis=1, tiled=True),
        lax.all_gather(values_local, "ctx", axis=1, tiled=True),
    )
    positions_all = keys_all.shape[1]
    key_valid = jnp.arange(positions_all) < IMG_TOK
    query_heads = query.reshape(slots, rows, heads_here, HD)

    def scores_with(key_block):
        key_heads = key_block.reshape(slots, positions_all, heads_here, HD)
        scores = (
            jnp.einsum(
                "srhe,sphe->shrp", query_heads, key_heads, preferred_element_type=jnp.float32
            )
            * score_scale
        )
        return jnp.where(key_valid[None, None, None, :], scores, -1e30)

    scores = scores_with(keys_all)
    row_peak = jnp.max(scores, axis=-1, keepdims=True)
    log_total = row_peak + jnp.log(jnp.sum(jnp.exp(scores - row_peak), axis=-1, keepdims=True))
    attn_prob = jnp.exp(scores - log_total).astype(jnp.bfloat16)
    value_heads = values_all.reshape(slots, positions_all, heads_here, HD)
    attended = (
        jnp.einsum("shrp,sphe->srhe", attn_prob, value_heads, preferred_element_type=jnp.float32)
        .astype(jnp.bfloat16)
        .reshape(count_rows, channels)
    )
    attn_part = matmul(attended, out_full)
    mixed = lax.psum(attn_part, "tp")
    after_attn = residual_in + mixed + biases[2]
    normed_b, normed_two, inv_two = normalize(after_attn, gains[1], biases[1])
    mlp_in = normed_b.astype(jnp.bfloat16)
    hidden_pre = matmul(mlp_in, fc1_full) + fc1_bias.astype(jnp.float32)
    hidden_act = gelu_tanh(hidden_pre).astype(jnp.bfloat16)
    mlp_part = matmul(hidden_act, fc2_full)
    mlp_total = lax.psum(mlp_part.astype(jnp.bfloat16), "tp").astype(jnp.float32)
    out_rows = ((after_attn + mlp_total + biases[3]) * row_mask).astype(jnp.bfloat16)
    grad_y = cotangent.reshape(count_rows, width).astype(jnp.float32) * row_mask
    grad_low = grad_y.astype(jnp.bfloat16)
    grad_fc2 = contract_rows(hidden_act, grad_low)
    grad_pre = contract_cols(grad_low, fc2_full) * gelu_slope(hidden_pre)
    grad_fc1_bias = jnp.sum(grad_pre, axis=0)
    grad_pre_bf = grad_pre.astype(jnp.bfloat16)
    grad_fc1 = contract_rows(mlp_in, grad_pre_bf)
    mlp_back_part = contract_cols(grad_pre_bf, fc1_full)
    grad_mlp_in = lax.psum(mlp_back_part, "tp")
    grad_after = grad_y + norm_back(grad_mlp_in, normed_two, inv_two, gains[1])
    grad_after_bf = grad_after.astype(jnp.bfloat16)
    layer_out = out_rows
    layer_out = layer_out.reshape(slots, rows, width)
    grad_out = contract_rows(attended, grad_after_bf)
    grad_attended = contract_cols(grad_after_bf, out_full).astype(jnp.bfloat16)
    keys_back, values_back = (keys_all, values_all)
    key_heads_back = keys_back.reshape(slots, positions_all, heads_here, HD)
    value_heads_back = values_back.reshape(slots, positions_all, heads_here, HD)
    grad_att_heads = grad_attended.reshape(slots, rows, heads_here, HD)
    delta = jnp.sum(
        grad_attended.astype(jnp.float32).reshape(slots, rows, heads_here, HD)
        * attended.astype(jnp.float32).reshape(slots, rows, heads_here, HD),
        axis=-1,
    )
    delta = jnp.transpose(delta, (0, 2, 1))[..., None]
    prob_back = jnp.exp(scores_with(keys_back) - log_total)
    grad_prob = jnp.einsum(
        "srhe,sphe->shrp", grad_att_heads, value_heads_back, preferred_element_type=jnp.float32
    )
    grad_scores = (prob_back * (grad_prob - delta)).astype(jnp.bfloat16)
    grad_query = (
        jnp.einsum(
            "shrp,sphe->srhe", grad_scores, key_heads_back, preferred_element_type=jnp.float32
        )
        * score_scale
    ).reshape(count_rows, channels)
    keys_part = (
        jnp.einsum("shrp,srhe->sphe", grad_scores, query_heads, preferred_element_type=jnp.float32)
        * score_scale
    ).reshape(slots, positions_all, channels)
    values_part = jnp.einsum(
        "shrp,srhe->sphe",
        prob_back.astype(jnp.bfloat16),
        grad_att_heads,
        preferred_element_type=jnp.float32,
    ).reshape(slots, positions_all, channels)
    grad_keys, grad_values = (
        lax.psum_scatter(keys_part, "ctx", scatter_dimension=1, tiled=True),
        lax.psum_scatter(values_part, "ctx", scatter_dimension=1, tiled=True),
    )
    grad_keys = grad_keys.reshape(count_rows, channels)
    grad_values = grad_values.reshape(count_rows, channels)
    grad_qv_bias = jnp.stack([jnp.sum(grad_query, axis=0), jnp.sum(grad_values, axis=0)])
    grad_stack = jnp.stack(
        [
            grad_query.astype(jnp.bfloat16),
            grad_keys.astype(jnp.bfloat16),
            grad_values.astype(jnp.bfloat16),
        ]
    )
    grad_qkv = jnp.einsum("nd,knc->kdc", attn_in, grad_stack, preferred_element_type=jnp.float32)
    attn_back_part = jnp.einsum(
        "knc,kdc->nd", grad_stack, qkv_full, preferred_element_type=jnp.float32
    )
    grad_attn_in = lax.psum(attn_back_part, "tp")
    normed_one_rows, inv_one_rows = (normed_one, inv_one)
    grad_token_rows = grad_after + norm_back(grad_attn_in, normed_one_rows, inv_one_rows, gains[0])
    grad_gains = jnp.stack(
        [jnp.sum(grad_attn_in * normed_one_rows, axis=0), jnp.sum(grad_mlp_in * normed_two, axis=0)]
    )
    grad_biases = jnp.stack(
        [
            jnp.sum(grad_attn_in, axis=0),
            jnp.sum(grad_mlp_in, axis=0),
            jnp.sum(grad_after, axis=0),
            jnp.sum(grad_y, axis=0),
        ]
    )
    grad_tokens = grad_token_rows
    grad_tokens = grad_tokens.reshape(slots, rows, width)
    shares = (
        lax.psum_scatter(grad_gains, "shard", scatter_dimension=1, tiled=True),
        lax.psum_scatter(grad_biases, "shard", scatter_dimension=1, tiled=True),
        lax.psum_scatter(grad_qkv, "shard", scatter_dimension=1, tiled=True),
        lax.psum_scatter(grad_out, "shard", scatter_dimension=1, tiled=True),
        lax.psum_scatter(grad_fc1, "shard", scatter_dimension=0, tiled=True),
        lax.psum_scatter(grad_fc2, "shard", scatter_dimension=1, tiled=True),
    )
    shares = lax.psum((shares[0], shares[1], shares[2], shares[3], shares[4], shares[5]), "ctx")
    gains_share, biases_share, qkv_share, out_share, fc1_share, fc2_share = shares
    qv_total, fc1_bias_total = lax.psum((grad_qv_bias, grad_fc1_bias), ("shard", "ctx"))
    return (
        layer_out,
        grad_tokens,
        gains_share,
        biases_share,
        qkv_share,
        qv_total,
        out_share,
        fc1_share,
        fc1_bias_total,
        fc2_share,
    )


def solution(mesh):
    placed = (
        P("shard", "ctx", None),
        P("shard"),
        P(None, "shard"),
        P(None, "shard"),
        P(None, "shard", "tp"),
        P(None, "tp"),
        P("tp", "shard"),
        P("shard", "tp"),
        P("tp"),
        P("tp", "shard"),
        P("shard", "ctx", None),
    )
    return jax.shard_map(
        per_device,
        mesh=mesh,
        in_specs=placed,
        out_specs=(
            P("shard", "ctx", None),
            P("shard", "ctx", None),
            P(None, "shard"),
            P(None, "shard"),
            P(None, "shard", "tp"),
            P(None, "tp"),
            P("tp", "shard"),
            P("shard", "tp"),
            P("tp"),
            P("tp", "shard"),
        ),
        check_vma=False,
    )
```

profile of v0, /device:TPU:0, one launch (start us, length us, event | category | flops | bytes accessed | tf_op | source)
XLA Modules:
  0.0 652.0 jit_solution(1075576584386723005)
XLA Ops:
  13.6 11.9 %all-gather = bf16[8,144,2]{1,2,0:T(2,128)(2,1)S(1)} all-gather(bf16[1,144,2]{1,2,0:T(2,128)(2,1)S(1)} %bitcast.197), channel_id=1, replica_groups=mesh['shard'=8,'ctx'=2,'tp'=8] {'shard'}, dimensions={0}, use_global_device_ids=true | all-gather | bytes 5184 | tf_op jit(solution)/shard_map/all_gather | solution.py:83
  25.6 11.2 %all-gather.1 = bf16[8,144,4]{1,2,0:T(4,128)(2,1)S(1)} all-gather(bf16[1,144,4]{1,2,0:T(4,128)(2,1)S(1)} %bitcast.196), channel_id=1, replica_groups=mesh['shard'=8,'ctx'=2,'tp'=8] {'shard'}, dimensions={0}, use_global_device_ids=true | all-gather | bytes 10368 | tf_op jit(solution)/shard_map/all_gather | solution.py:84
  37.3 14.3 %all_gather.29 = bf16[144,1152]{0,1:T(8,128)(2,1)} all-gather(bf16[144,144]{0,1:T(8,128)(2,1)S(1)} %copy.48), channel_id=1, replica_groups=mesh['shard'=8,'ctx'=2,'tp'=8] {'shard'}, dimensions={1}, use_global_device_ids=true | all-gather | bytes 373248 | tf_op jit(solution)/shard_map/all_gather | solution.py:80
  51.5 17.9 %all_gather.26 = bf16[3,1152,144]{2,0,1:T(4,128)(2,1)} all-gather(bf16[3,144,144]{2,0,1:T(4,128)(2,1)S(1)} %copy.42), channel_id=1, replica_groups=mesh['shard'=8,'ctx'=2,'tp'=8] {'shard'}, dimensions={1}, use_global_device_ids=true | all-gather | bytes 1119744 | tf_op jit(solution)/shard_map/all_gather | solution.py:79
  69.4 4.0 copy.43
  75.9 13.2 %all_gather.28 = bf16[1,736,144]{2,0,1:T(2,128)(2,1)S(1)} all-gather(bf16[1,368,144]{2,0,1:T(2,128)(2,1)S(1)} %copy.46), channel_id=1, replica_groups=mesh['shard'=8,'ctx'=2,'tp'=8] {'ctx'}, dimensions={1}, use_global_device_ids=true | all-gather | bytes 317952 | tf_op jit(solution)/shard_map/all_gather | solution.py:97
  90.7 12.4 %all_gather.27 = bf16[1,736,144]{2,0,1:T(2,128)(2,1)S(1)} all-gather(bf16[1,368,144]{2,0,1:T(2,128)(2,1)S(1)} %copy.44), channel_id=1, replica_groups=mesh['shard'=8,'ctx'=2,'tp'=8] {'ctx'}, dimensions={1}, use_global_device_ids=true | all-gather | bytes 317952 | tf_op jit(solution)/shard_map/all_gather | solution.py:98
  112.1 78.3 %all-reduce.9.cloned.1.call-done = f32[368,1152]{1,0:T(8,128)} async-done(((f32[368,1152]{1,0:T(8,128)}), f32[368,1152]{1,0:T(8,128)}) %all-reduce.9.cloned.1.call-update) | async-done | bytes 1695760 | tf_op jit(solution)/shard_map/psum | solution.py:125
  193.7 4.0 convolution_add_fusion
  197.7 3.7 fusion.59
  202.2 2.2 fusion.42
  204.6 3.6 convolution_convert_fusion
  208.3 76.1 %all-reduce.13.cloned.1.call-done = f32[368,1152]{1,0:T(8,128)} async-done(((f32[368,1152]{1,0:T(8,128)}), f32[368,1152]{1,0:T(8,128)}) %all-reduce.13.cloned.1.call-update) | async-done | bytes 1695760 | tf_op jit(solution)/shard_map/psum | solution.py:142
  284.4 2.7 multiply_reduce_fusion
  287.0 76.2 %all-reduce.11.cloned.1.call-done = bf16[368,1152]{1,0:T(8,128)(2,1)} async-done(((bf16[368,1152]{1,0:T(8,128)(2,1)}), bf16[368,1152]{1,0:T(8,128)(2,1)}) %all-reduce.11.cloned.1.call-update) | async-done | bytes 847888 | tf_op jit(solution)/shard_map/psum | solution.py:132
  363.3 4.8 fusion.52
  369.9 2.5 copy.53
  378.6 15.5 %reduce-scatter.27.cloned.1.call-done = f32[368,144]{1,0:T(8,128)} async-done(((f32[736,144]{1,0:T(8,128)}), f32[368,144]{1,0:T(8,128)}) %reduce-scatter.27.cloned.1.call-update) | async-done | bytes 211984
  396.8 20.2 %reduce-scatter.25.cloned.1.call-done = f32[368,144]{1,0:T(8,128)} async-done(((f32[736,144]{1,0:T(8,128)}), f32[368,144]{1,0:T(8,128)}) %reduce-scatter.25.cloned.1.call-update) | async-done | bytes 211984
  424.0 2.3 convolution_bitcast_fusion
  426.3 5.5 copy.59
  431.7 6.2 reshape.258
  439.4 3.9 fusion.40
  444.8 2.9 fusion.32
  448.5 52.3 %all-reduce.15.cloned.1.call-done = f32[368,1152]{1,0:T(8,128)} async-done(((f32[368,1152]{1,0:T(8,128)}), f32[368,1152]{1,0:T(8,128)}) %all-reduce.15.cloned.1.call-update) | async-done | bytes 1695760 | tf_op jit(solution)/shard_map/psum | solution.py:198
  500.8 2.5 fusion.16
  505.7 37.4 %all-reduce = (f32[2,144]{1,0:T(2,128)}, f32[538]{0:T(1024)}) all-reduce(f32[2,144]{1,0:T(2,128)S(1)} %pad_maximum_fusion.5, f32[538]{0:T(1024)S(1)} %copy-done.45), channel_id=1, replica_groups=mesh['shard'=8,'ctx'=2,'tp'=8] {'shard','ctx'}, use_global_device_ids=true, to_apply=%region_31.32 | all-reduce | flops 826 | bytes 6608 | tf_op jit(solution)/shard_map/psum | solution.py:224
  547.1 18.4 %reduce-scatter.23.cloned.1.call-done = f32[538,144]{0,1:T(8,128)} async-done(((f32[538,1152]{0,1:T(8,128)}), f32[538,144]{0,1:T(8,128)}) %reduce-scatter.23.cloned.1.call-update) | async-done | bytes 309904 | tf_op jit(solution)/shard_map/reduce_scatter | solution.py:220
  565.5 3.2 fusion.15
  568.8 29.5 %reduce-scatter.29.cloned.1.call-done = f32[144,2]{1,0:T(8,128)} async-done(((f32[1152,2]{1,0:T(8,128)}), f32[144,2]{1,0:T(8,128)}) %reduce-scatter.29.cloned.1.call-update) | async-done | bytes 1168
  599.2 31.2 %reduce-scatter.31.cloned.1.call-done = f32[144,4]{1,0:T(8,128)} async-done(((f32[1152,4]{1,0:T(8,128)}), f32[144,4]{1,0:T(8,128)}) %reduce-scatter.31.cloned.1.call-update) | async-done | bytes 2320
  631.3 7.1 %all-reduce.1 = (f32[2,144]{1,0:T(2,128)}, f32[4,144]{1,0:T(4,128)}) all-reduce(f32[2,144]{1,0:T(2,128)S(1)} %copy.56, f32[4,144]{1,0:T(4,128)S(1)} %copy.58), channel_id=1, replica_groups=mesh['shard'=8,'ctx'=2,'tp'=8] {'ctx'}, use_global_device_ids=true, to_apply=%region_20.21 | all-reduce | flops 864 | bytes 6912 | tf_op jit(solution)/shard_map/psum | solution.py:222
  (208 shorter events, 58.1 us)
Async XLA Ops:
  8.0 5.6 copy-start.48
  8.0 17.6 %copy-start.46 = (bf16[4,144]{1,0:T(4,128)(2,1)S(1)}, bf16[4,144]{1,0:T(4,128)(2,1)}, u32[]{:S(2)}) copy-start(bf16[4,144]{1,0:T(4,128)(2,1)} %param.14) | copy-start | bytes 3460
  8.0 28.9 %copy-start.29 = (bf16[144,144]{1,0:T(8,128)(2,1)S(1)}, bf16[144,144]{1,0:T(8,128)(2,1)}, u32[]{:S(2)}) copy-start(bf16[144,144]{1,0:T(8,128)(2,1)} %param.17) | copy-start | bytes 124420
  8.0 29.0 %copy-start.25 = (bf16[3,144,144]{2,1,0:T(8,128)(2,1)S(1)}, bf16[3,144,144]{2,1,0:T(8,128)(2,1)}, u32[]{:S(2)}) copy-start(bf16[3,144,144]{2,1,0:T(8,128)(2,1)} %param.15) | copy-start | bytes 373252
  8.1 182.3 %all-reduce.9.cloned.1.call-start = ((), (), s32[]{:S(2)}) async-start(), calls=%async_computation.8 | async-start | bytes 3391488 | tf_op jit(solution)/shard_map/psum | solution.py:125
  13.6 60.6 %copy-start.35 = (f32[368]{0:T(512)}, f32[368]{0:T(512)S(1)}, u32[]{:S(2)}) copy-start(f32[368]{0:T(512)S(1)} %add_rsqrt_fusion.1) | copy-start | bytes 4420
  69.4 4.8 copy-start.4
  75.2 29.6 %copy-start.11 = (f32[1,368,144]{1,2,0:T(8,128)}, f32[1,368,144]{1,2,0:T(8,128)S(1)}, u32[]{:S(2)}) copy-start(f32[1,368,144]{1,2,0:T(8,128)S(1)} %get-tuple-element.80) | copy-start | bytes 635908
  90.0 16.2 %copy-start.13 = (bf16[1,736,144]{1,2,0:T(8,128)(2,1)}, bf16[1,736,144]{1,2,0:T(8,128)(2,1)S(1)}, u32[]{:S(2)}) copy-start(bf16[1,736,144]{1,2,0:T(8,128)(2,1)S(1)} %copy.47) | copy-start | bytes 635908
  108.5 81.9 %copy-start.31 = (f32[1152]{0:T(1024)S(1)}, f32[1152]{0:T(1024)}, u32[]{:S(2)}) copy-start(f32[1152]{0:T(1024)} %get-tuple-element.60) | copy-start | bytes 13828
  110.1 83.5 %all-gather.5.cloned.1.call-start = ((), (), s32[]{:S(2)}) async-start(), calls=%async_computation.9 | async-start | bytes 1658880 | tf_op jit(solution)/shard_map/all_gather | solution.py:81
  110.7 86.9 %all-gather.7.cloned.1.call-start = ((), (), s32[]{:S(2)}) async-start(), calls=%async_computation.10 | async-start | bytes 1658880 | tf_op jit(solution)/shard_map/all_gather | solution.py:82
  111.3 173.1 %all-reduce.13.cloned.1.call-start = ((), (), s32[]{:S(2)}) async-start(), calls=%async_computation.12 | async-start | bytes 3391488 | tf_op jit(solution)/shard_map/psum | solution.py:142
  112.1 251.2 %copy-start.38 = (f32[368]{0:T(512)}, f32[368]{0:T(512)S(1)}, u32[]{:S(2)}) copy-start(f32[368]{0:T(512)S(1)} %fusion.45) | copy-start | bytes 4420
  197.7 4.5 copy-start.20
  204.4 158.9 %all-reduce.11.cloned.1.call-start = ((), (), s32[]{:S(2)}) async-start(), calls=%async_computation.11 | async-start | bytes 1695744 | tf_op jit(solution)/shard_map/psum | solution.py:132
  208.2 155.0 %copy-start.32 = (f32[1152]{0:T(1024)S(1)}, f32[1152]{0:T(1024)}, u32[]{:S(2)}) copy-start(f32[1152]{0:T(1024)} %get-tuple-element.58) | copy-start | bytes 13828
  208.3 185.9 %reduce-scatter.27.cloned.1.call-start = ((), (), s32[]{:S(2)}) async-start(), calls=%async_computation.17 | async-start | bytes 1130496
  363.3 4.8 copy-start.8
  373.3 43.8 %reduce-scatter.25.cloned.1.call-start = ((), (), s32[]{:S(2)}) async-start(), calls=%async_computation.16 | async-start | bytes 1130496
  377.4 41.5 %copy-start.22 = (bf16[3,1152,144]{1,2,0:T(8,128)(2,1)S(1)}, bf16[3,1152,144]{1,2,0:T(8,128)(2,1)}, u32[]{:S(2)}) copy-start(bf16[3,1152,144]{1,2,0:T(8,128)(2,1)} %copy-done.21) | copy-start | bytes 2985988
  377.4 123.3 %all-reduce.15.cloned.1.call-start = ((), (), s32[]{:S(2)}) async-start(), calls=%async_computation.13 | async-start | bytes 3391488 | tf_op jit(solution)/shard_map/psum | solution.py:198
  421.0 122.1 %reduce-scatter.35.cloned.1.call-start = ((), (), s32[]{:S(2)}) async-start(), calls=%async_computation.21 | async-start | bytes 1327104
  423.9 120.8 %reduce-scatter.33.cloned.1.call-start = ((), (), s32[]{:S(2)}) async-start(), calls=%async_computation.20 | async-start | bytes 2654208
  438.0 109.2 %reduce-scatter.21.cloned.1.call-start = ((), (), s32[]{:S(2)}) async-start(), calls=%async_computation.14 | async-start | bytes 3317760 | tf_op jit(solution)/shard_map/reduce_scatter | solution.py:219
  443.4 122.1 %reduce-scatter.23.cloned.1.call-start = ((), (), s32[]{:S(2)}) async-start(), calls=%async_computation.15 | async-start | bytes 3317760 | tf_op jit(solution)/shard_map/reduce_scatter | solution.py:220
  447.7 53.1 %copy-start.6 = (bf16[1,368,1152]{2,1,0:T(8,128)(2,1)S(1)}, bf16[1,368,1152]{2,1,0:T(8,128)(2,1)}, u32[]{:S(2)}) copy-start(bf16[1,368,1152]{2,1,0:T(8,128)(2,1)} %param.11) | copy-start | bytes 2543620
  447.7 53.1 %copy-start.37 = (f32[368]{0:T(512)S(1)}, f32[368]{0:T(512)}, u32[]{:S(2)}) copy-start(f32[368]{0:T(512)} %copy-done.35) | copy-start | bytes 4420
  447.7 150.5 %reduce-scatter.29.cloned.1.call-start = ((), (), s32[]{:S(2)}) async-start(), calls=%async_computation.18 | async-start | bytes 663552
  504.4 126.0 %reduce-scatter.31.cloned.1.call-start = ((), (), s32[]{:S(2)}) async-start(), calls=%async_computation.19 | async-start | bytes 663552
  505.6 132.8 %all-reduce.17.cloned.1.call-start = ((), (), s32[]{:S(2)}) async-start(), calls=%async_computation.22 | async-start | bytes 2654208 | tf_op jit(solution)/shard_map/psum | solution.py:222
  638.4 5.4 copy-start.24
  (32 other events, 58.2 us)
Sparse Core Ops, SparseCore 0:
  110.3 80.0 all-reduce.8
  204.5 79.8 all-reduce.12
  287.5 75.7 all-reduce.10
  373.4 20.6 reduce-scatter.26
  396.5 20.5 reduce-scatter.24
  421.0 79.6 all-reduce.14
  565.6 53.3 all-reduce.16
Sparse Core Ops, SparseCore 1:
  112.4 24.2 all-gather.4
  138.3 24.4 all-gather.6
  424.0 32.6 reduce-scatter.34
  459.1 33.0 reduce-scatter.32
  494.6 34.4 reduce-scatter.20
  531.6 33.8 reduce-scatter.22
  567.7 30.4 reduce-scatter.28
  600.5 29.8 reduce-scatter.30
where the time goes:
time: 653 us; the launch traced here: 652 us
  waiting for transfers between devices  399 us (61%)
  blocking collectives  125 us (19%)
  local copies, waits for them, and re-layouts  51.8 us (8%)
  matrix products  35.4 us (5%)
  other arithmetic  22.2 us (3%)
  between operations  17.1 us (3%)
    unnamed x21, waiting for transfers between devices  97.7 us
    psum x1, waiting for transfers between devices, per_device(): mixed = lax.psum(attn_part, 'tp')  78.3 us
    psum x1, waiting for transfers between devices, per_device(): lax.psum(mlp_part.astype(jnp.bfloat16), 'tp').astype(jnp.float32)  76.2 us
    psum x1, waiting for transfers between devices, per_device(): grad_mlp_in = lax.psum(mlp_back_part, 'tp')  76.1 us
    psum x1, waiting for transfers between devices, per_device(): grad_attn_in = lax.psum(attn_back_part, 'tp')  52.3 us
    unnamed x120, local copies, waits for them, and re-layouts  41.5 us
    psum x1, blocking collectives, per_device(): lax.psum((grad_qv_bias, grad_fc1_bias), ('shard', 'ctx'))  37.4 us
    reduce_scatter x1, waiting for transfers between devices, per_device(): lax.psum_scatter(grad_fc2, 'shard', scatter_dimension=1, tiled=True)  18.4 us
  transfers between devices with their start and end apart: 15, of which 9 were waited for; matrix products, arithmetic and copies ran while one was open for 9% of the time, Pallas kernels for 0%

commit v1 on v0

v1 whole, which is shorter than its diff:
```python
import math

import jax
import jax.numpy as jnp
from jax import lax
from jax.experimental import pallas as pl
from jax.experimental.pallas import tpu as pltpu
from jax.sharding import PartitionSpec as P

HD = 72
IMG_TOK = 729
EPS = 1e-06
GELU_C = math.sqrt(2.0 / math.pi)
GELU_A = 0.044715
SCALE = HD ** (-0.5)

D = 1152
ROWS = 368
PAD = 384
OWN = 48
BLK = 144
LN = 640
FF_OWN = 538
CH = 96

MESH = pl.DeviceIdType.MESH
F32 = jnp.float32
BF = jnp.bfloat16


def nn(a, b):
    return jnp.dot(a, b, preferred_element_type=F32)


def nt(a, b):
    return lax.dot_general(a, b, (((1,), (1,)), ((), ())), preferred_element_type=F32)


def tn(a, b):
    return lax.dot_general(a, b, (((0,), (0,)), ((), ())), preferred_element_type=F32)


def mean_rows(x):
    return jnp.sum(x, axis=-1, keepdims=True) * (1.0 / D)


def rcopy(src, dst, send, recv, dev):
    return pltpu.make_async_remote_copy(
        src_ref=src,
        dst_ref=dst,
        send_sem=send,
        recv_sem=recv,
        device_id=dev,
        device_id_type=MESH,
    )


def rows_at(start, size, unit=16):
    if not isinstance(start, int):
        start = pl.multiple_of(start, unit)
    return pl.ds(start, size)


def layer_kernel(
    count,
    tok,
    cot,
    wa_in,
    wb_in,
    wc_in,
    bias_rows,
    out_ref,
    gtok_ref,
    ga_ref,
    gb_ref,
    gc_ref,
    vec_ref,
    small_ref,
    wa,
    wb,
    wc,
    tokp,
    glow,
    attin,
    qh,
    kvo,
    kvx,
    sel,
    sela,
    prob,
    att,
    atth,
    part1,
    part2,
    part3,
    part4,
    rr1,
    rr2,
    rr3,
    rr4,
    g1,
    g2,
    g3,
    g4,
    gp0,
    hid,
    gpb,
    xh2,
    aft,
    r2s,
    gao,
    vrows,
    vecg,
    fulla,
    fullb,
    fullc,
    xs,
    xr,
    zs,
    zr,
    cs,
    cr,
    totb,
    dks,
    dkr,
    dkown,
    dqb,
    dsb,
    pbf,
    gah,
    gs,
    smx,
    smz,
    smc,
    vt,
    wz_s,
    wz_r,
    wc_s,
    wc_r,
    kv_s,
    kv_r,
    dk_s,
    dk_r,
    rs_s,
    rs_r,
    ag_s,
    ag_r,
    x_s,
    x_r,
    z_s,
    z_r,
    c_s,
    c_r,
    sx_s,
    sx_r,
    sz_s,
    sz_r,
    sc_s,
    sc_r,
    v_s,
    v_r,
):
    s = lax.axis_index("shard")
    c = lax.axis_index("ctx")
    t = lax.axis_index("tp")
    z = s // 2
    core = lax.rem(s, 2)
    sib = {"shard": z * 2 + 1 - core}
    octx = {"ctx": 1 - c}

    def zdev(zz):
        return {"shard": zz * 2 + core}

    def zoff(d):
        return lax.rem(z + d + 4, 4)

    def tpd(d):
        return lax.rem(t + d, 8)

    pending = []

    bar = pltpu.get_barrier_semaphore()
    for d in range(1, 8):
        pl.semaphore_signal(bar, inc=1, device_id={"tp": tpd(d)}, device_id_type=MESH)
    for d in range(1, 4):
        pl.semaphore_signal(bar, inc=1, device_id=zdev(zoff(d)), device_id_type=MESH)
    pl.semaphore_signal(bar, inc=1, device_id=sib, device_id_type=MESH)
    pl.semaphore_signal(bar, inc=1, device_id=octx, device_id_type=MESH)
    pl.semaphore_wait(bar, 12)

    groups = ((wa_in, wa), (wb_in, wb), (wc_in, wc))

    def block(ref, idx):
        return ref.at[rows_at(idx * BLK, BLK)]

    def w_start(g):
        src, full = groups[g]
        for d in (2, 1, 3):
            cp = rcopy(src, block(full, s), wz_s.at[g, d - 1], wz_r.at[g, d - 1], zdev(zoff(d)))
            cp.start()
            pending.append(cp)
        cp = rcopy(src, block(full, s), wc_s.at[g, 0], wc_r.at[g, 0], sib)
        cp.start()
        pending.append(cp)
        full[rows_at(s * BLK, BLK), :] = src[...]

    def w_forward(g):
        full = groups[g][1]
        for d in (1, 3, 2):
            got = block(full, zoff(-d) * 2 + core)
            rcopy(got, got, wz_s.at[g, d - 1], wz_r.at[g, d - 1], sib).wait_recv()
            cp = rcopy(got, got, wc_s.at[g, d], wc_r.at[g, d], sib)
            cp.start()
            pending.append(cp)

    def w_wait(g):
        full = groups[g][1]
        for d in range(4):
            got = block(full, zoff(-d) * 2 + 1 - core)
            rcopy(got, got, wc_s.at[g, d], wc_r.at[g, d], sib).wait_recv()

    w_start(0)

    def rs_send(k, part, rr, j):
        @pl.when(j != t)
        def _():
            rcopy(
                part.at[rows_at(j * OWN, OWN)], rr.at[t], rs_s.at[k, j], rs_r.at[k, t], {"tp": j}
            ).start()

    def rs_chunk(i):
        return lax.rem(t // 2 + 1 + i, 4)

    def rs_sum(k, part, rr):
        total = part[rows_at(t * OWN, OWN), :].astype(F32)
        for d in range(1, 8):
            j = tpd(d)
            rcopy(rr.at[j], rr.at[j], rs_s.at[k, j], rs_r.at[k, j], {"tp": j}).wait_recv()
            total = total + rr[j].astype(F32)
        return total

    def rs_done(k, part, rr):
        for d in range(1, 8):
            j = tpd(d)
            rcopy(
                part.at[rows_at(j * OWN, OWN)], rr.at[t], rs_s.at[k, j], rs_r.at[k, t], {"tp": j}
            ).wait_send()

    def ag_start(k, buf):
        mine = buf.at[rows_at(t * OWN, OWN)]
        for d in range(1, 8):
            cp = rcopy(mine, mine, ag_s.at[k, d], ag_r.at[k, t], {"tp": tpd(d)})
            cp.start()
            pending.append(cp)

    def ag_wait_block(k, buf, j):
        @pl.when(j != t)
        def _():
            blk = buf.at[rows_at(j * OWN, OWN)]
            rcopy(blk, blk, ag_s.at[k, 0], ag_r.at[k, j], {"tp": j}).wait_recv()

    def ag_wait(k, buf):
        for d in range(1, 8):
            j = tpd(d)
            blk = buf.at[rows_at(j * OWN, OWN)]
            rcopy(blk, blk, ag_s.at[k, 0], ag_r.at[k, j], {"tp": j}).wait_recv()

    row_i = lax.broadcasted_iota(jnp.int32, (128, 512), 0)
    lane_i = lax.broadcasted_iota(jnp.int32, (128, 512), 1)
    for j in range(6):
        hit = (lane_i == row_i + (16 + HD * j)) & (row_i < HD)
        sel[128 * j : 128 * j + 128, :] = jnp.where(hit, 1.0, 0.0).astype(BF)
    row_h = lax.broadcasted_iota(jnp.int32, (128, 256), 0)
    lane_h = lax.broadcasted_iota(jnp.int32, (128, 256), 1)
    for j in range(2):
        hit = (lane_h == row_h + HD * j) & (row_h < HD)
        sela[128 * j : 128 * j + 128, :] = jnp.where(hit, 1.0, 0.0).astype(BF)

    live = jnp.where(count[0] > 0, 1.0, 0.0)
    limit = IMG_TOK - c * ROWS

    def mask_at(start, size):
        pos = lax.broadcasted_iota(jnp.int32, (size, 1), 0) + start
        return jnp.where(pos < jnp.minimum(limit, ROWS), live, 0.0)

    def stats(x):
        centred = x - mean_rows(x)
        inv = lax.rsqrt(mean_rows(centred * centred) + EPS)
        return centred * inv, inv

    def prep(i, _):
        at = rows_at(i * 16, 16)
        tokp[at, :] = tok[at, :]
        glow[at, :] = (cot[at, :].astype(F32) * mask_at(i * 16, 16)).astype(BF)
        return 0

    lax.fori_loop(0, ROWS // 16, prep, 0)
    tokp[ROWS:PAD, :] = jnp.zeros((PAD - ROWS, D), BF)
    glow[ROWS:PAD, :] = jnp.zeros((PAD - ROWS, D), BF)
    vecg[...] = jnp.zeros_like(vecg)

    w_forward(0)
    w_wait(0)
    w_start(1)
    vrows[...] = wa[:, 512:640].astype(F32).T
    gain0 = vrows[64:65, :]
    gain1 = vrows[65:66, :]
    bias0 = vrows[66:67, :]
    bias1 = vrows[67:68, :]
    bias2 = vrows[68:69, :]
    bias3 = vrows[69:70, :]

    def norm_one(i, _):
        at = rows_at(i * 48, 48)
        normed, _inv = stats(tokp[at, :].astype(F32))
        attin[at, :] = (normed * gain0 + bias0).astype(BF)
        return 0

    lax.fori_loop(0, 8, norm_one, 0)

    def project(i, _):
        at = rows_at(i * 128, 128)
        low = (nn(attin[at, :], wa[:, 128:640]) + bias_rows[0:1, 0:512]).astype(BF)
        heads = nt(low, sel[...]).astype(BF)
        for j in range(2):
            qh[j, at, :] = heads[:, 128 * j : 128 * j + 128]
        for j in range(4):
            kvo[j, at, :] = heads[:, 256 + 128 * j : 384 + 128 * j]
        return 0

    lax.fori_loop(0, 3, project, 0)
    for j in range(4):
        cp = rcopy(kvo.at[j], kvx.at[j], kv_s.at[j], kv_r.at[j], octx)
        cp.start()
        pending.append(cp)

    lane_k = lax.broadcasted_iota(jnp.int32, (128, PAD), 1)
    own_keys = jnp.minimum(limit, ROWS)
    other_keys = jnp.minimum(IMG_TOK - (1 - c) * ROWS, ROWS)

    def own_scores(i, _):
        at = rows_at(i * 128, 128)
        for h in range(2):
            sc = nt(qh[h, at, :], kvo[h]) * SCALE
            prob[h, at, 0:PAD] = jnp.where(lane_k < own_keys, sc, -1e30)
        return 0

    lax.fori_loop(0, 3, own_scores, 0)
    w_forward(1)
    w_start(2)
    for j in range(4):
        rcopy(kvo.at[j], kvx.at[j], kv_s.at[j], kv_r.at[j], octx).wait_recv()

    def attend(i, _):
        at = rows_at(i * 128, 128)
        lows = []
        for h in range(2):
            sc = nt(qh[h, at, :], kvx[h]) * SCALE
            sc = jnp.where(lane_k < other_keys, sc, -1e30)
            so = prob[h, at, 0:PAD]
            peak = jnp.maximum(
                jnp.max(sc, axis=-1, keepdims=True), jnp.max(so, axis=-1, keepdims=True)
            )
            eo = jnp.exp(so - peak)
            ex = jnp.exp(sc - peak)
            inv = 1.0 / (
                jnp.sum(eo, axis=-1, keepdims=True) + jnp.sum(ex, axis=-1, keepdims=True)
            )
            po = eo * inv
            px = ex * inv
            prob[h, at, 0:PAD] = po
            prob[h, at, PAD : 2 * PAD] = px
            pol = po.astype(BF)
            pxl = px.astype(BF)
            pbf[h, at, 0:PAD] = pol
            pbf[h, at, PAD : 2 * PAD] = pxl
            low = (nn(pol, kvo[2 + h]) + nn(pxl, kvx[2 + h])).astype(BF)
            atth[h, at, :] = low
            lows.append(low)
        packed = nn(lows[0], sela[0:128, :]) + nn(lows[1], sela[128:256, :])
        att[at, :] = packed.astype(BF)
        return 0

    lax.fori_loop(0, 3, attend, 0)

    def out_proj(i, _):
        ch = rs_chunk(i)
        at = rows_at(ch * CH, CH)
        part1[at, :] = nt(att[at, :], wa[:, 0:256]).astype(BF)
        for b in range(2):
            rs_send(0, part1, rr1, ch * 2 + b)
        return 0

    lax.fori_loop(0, 4, out_proj, 0)
    w_wait(1)
    w_forward(2)
    w_wait(2)

    def fc2_back(i, _):
        at = rows_at(i * 128, 128)
        gp0[at, :] = nn(glow[at, :], wc[...])
        return 0

    lax.fori_loop(0, 3, fc2_back, 0)

    own = rows_at(t * OWN, OWN)
    after = tokp[own, :].astype(F32) + rs_sum(0, part1, rr1) + bias2
    aft[...] = after
    normed_two, inv_two = stats(after)
    xh2[...] = normed_two
    r2s[...] = jnp.broadcast_to(inv_two, (OWN, 128))
    g1[own, :] = (normed_two * gain1 + bias1).astype(BF)
    ag_start(0, g1)

    def mlp(i, colsum):
        ch = lax.rem(t // 2 + i, 4)
        at = rows_at(ch * CH, CH)
        for b in range(2):
            ag_wait_block(0, g1, ch * 2 + b)
        u = nn(g1[at, :], wb[...]) + bias_rows[1:2, :]
        uu = u * u
        tang = jnp.tanh(GELU_C * u * (1.0 + GELU_A * uu))
        hid[at, :] = (0.5 * u * (1.0 + tang)).astype(BF)
        slope = 0.5 * (1.0 + tang) + (0.5 * GELU_C) * u * (1.0 - tang * tang) * (
            1.0 + 3.0 * GELU_A * uu
        )
        gpre = gp0[at, :] * slope
        low = gpre.astype(BF)
        gpb[at, :] = low
        part2[at, :] = nt(low, wb[...]).astype(BF)
        for b in range(2):
            rs_send(1, part2, rr2, ch * 2 + b)
        return colsum + jnp.sum(gpre, axis=0, keepdims=True)

    fc1_sum = lax.fori_loop(0, 4, mlp, jnp.zeros((1, LN), F32))

    def fc2_fwd(i, _):
        at = rows_at(i * CH, CH)
        part3[at, :] = nt(hid[at, :], wc[...]).astype(BF)
        return 0

    def grad_full(full, left, right):
        for k in range(3):
            full[384 * k : 384 * k + 384, :] = tn(left[:, 384 * k : 384 * k + 384], right[...])

    def x_start(g, full):
        for zz in range(4):
            xs[g, zz] = full[rows_at((2 * zz + 1 - core) * BLK, BLK), :].astype(BF)
        cp = rcopy(xs.at[g], xr.at[g], x_s.at[g], x_r.at[g], sib)
        cp.start()
        pending.append(cp)

    def z_start(g, full):
        rcopy(xs.at[g], xr.at[g], x_s.at[g], x_r.at[g], sib).wait_recv()
        for d in (2, 1, 3):
            zz = zoff(d)
            zs[g, zz] = (
                full[rows_at((2 * zz + core) * BLK, BLK), :] + xr[g, zz].astype(F32)
            ).astype(BF)
            cp = rcopy(zs.at[g, zz], zr.at[g, d], z_s.at[g, d], z_r.at[g, d], zdev(zz))
            cp.start()
            pending.append(cp)

    def c_start(g, full):
        total = full[rows_at((2 * z + core) * BLK, BLK), :] + xr[g, z].astype(F32)
        for d in range(1, 4):
            rcopy(zs.at[g, 0], zr.at[g, d], z_s.at[g, d], z_r.at[g, d], zdev(zoff(d))).wait_recv()
            total = total + zr[g, d].astype(F32)
        cs[g] = total.astype(BF)
        cp = rcopy(cs.at[g], cr.at[g], c_s.at[g], c_r.at[g], octx)
        cp.start()
        pending.append(cp)

    def c_finish(g, ref):
        rcopy(cs.at[g], cr.at[g], c_s.at[g], c_r.at[g], octx).wait_recv()
        ref[...] = cs[g].astype(F32) + cr[g].astype(F32)

    grad_full(fullc, glow, hid)
    x_start(2, fullc)
    lax.fori_loop(0, 4, fc2_fwd, 0)

    g_mlp = rs_sum(1, part2, rr2)
    scaled = g_mlp * gain1
    normed_two = xh2[...]
    grad_y = glow[own, :].astype(F32)
    grad_after = grad_y + r2s[:, 0:1] * (
        scaled - mean_rows(scaled) - normed_two * mean_rows(scaled * normed_two)
    )
    gao[...] = grad_after
    g2[own, :] = grad_after.astype(BF)
    ag_start(1, g2)
    vecg[65:66, :] = jnp.sum(g_mlp * normed_two, axis=0, keepdims=True)
    vecg[67:68, :] = jnp.sum(g_mlp, axis=0, keepdims=True)
    vecg[68:69, :] = jnp.sum(grad_after, axis=0, keepdims=True)
    vecg[69:70, :] = jnp.sum(grad_y, axis=0, keepdims=True)

    z_start(2, fullc)
    grad_full(fullb, g1, gpb)
    x_start(1, fullb)

    ag_wait(1, g2)
    for j in range(8):
        rs_send(2, part3, rr3, lax.rem(t + j, 8))
    z_start(1, fullb)

    def grad_att(i, _):
        at = rows_at(i * 128, 128)
        low = nn(g2[at, :], wa[:, 0:256]).astype(BF)
        heads = nt(low, sela[...]).astype(BF)
        for h in range(2):
            gah[h, at, :] = heads[:, 128 * h : 128 * h + 128]
        return 0

    lax.fori_loop(0, 3, grad_att, 0)

    q_sums = []
    for h in range(2):

        def back(i, acc, h=h):
            at = rows_at(i * 128, 128)
            gh = gah[h, at, :]
            delta = jnp.sum(gh.astype(F32) * atth[h, at, :].astype(F32), axis=-1, keepdims=True)
            dso = (prob[h, at, 0:PAD] * (nt(gh, kvo[2 + h]) - delta)).astype(BF)
            dsx = (prob[h, at, PAD : 2 * PAD] * (nt(gh, kvx[2 + h]) - delta)).astype(BF)
            dsb[h, at, 0:PAD] = dso
            dsb[h, at, PAD : 2 * PAD] = dsx
            dq = (nn(dso, kvo[h]) + nn(dsx, kvx[h])) * SCALE
            dqb[at, 128 * h : 128 * h + 128] = dq.astype(BF)
            return acc + jnp.sum(dq, axis=0, keepdims=True)

        q_sums.append(lax.fori_loop(0, 3, back, jnp.zeros((1, 128), F32)))

    for h in range(2):
        for which, left, right in ((h, qh, dsb), (2 + h, gah, pbf)):
            grad = tn(left[h], right[h])
            if which < 2:
                grad = grad * SCALE
            dks[which] = grad[0:80, PAD : 2 * PAD].astype(BF)
            dkown[which] = grad[:, 0:PAD]
            cp = rcopy(dks.at[which], dkr.at[which], dk_s.at[which], dk_r.at[which], octx)
            cp.start()
            pending.append(cp)

    c_start(2, fullc)
    for k in range(3):
        fulla[384 * k : 384 * k + 384, 0:256] = tn(g2[:, 384 * k : 384 * k + 384], att[...])
    lay = (aft[...] + rs_sum(2, part3, rr3) + bias3) * mask_at(t * OWN, OWN)
    g3[own, :] = lay.astype(BF)

    for j in range(4):
        rcopy(dks.at[j], dkr.at[j], dk_s.at[j], dk_r.at[j], octx).wait_recv()
        totb[128 * j : 128 * j + 80, :] = (dkown[j, 0:80, :] + dkr[j].astype(F32)).astype(BF)
        totb[128 * j + 80 : 128 * j + 128, :] = jnp.zeros((48, PAD), BF)

    gs[...] = (nn(dqb[...], sel[0:256, :]) + tn(totb[...], sel[256:768, :])).astype(BF)

    def qkv_back(i, acc):
        ch = rs_chunk(i)
        at = rows_at(ch * CH, CH)
        grad = nt(gs[at, :], wa[:, 128:640])
        part4[at, :] = grad.astype(BF)
        for b in range(2):
            rs_send(3, part4, rr4, ch * 2 + b)
        normed, _inv = stats(tokp[at, :].astype(F32))
        return (
            acc[0] + jnp.sum(grad * normed, axis=0, keepdims=True),
            acc[1] + jnp.sum(grad, axis=0, keepdims=True),
        )

    zero_row = jnp.zeros((1, D), F32)
    gain_sum, bias_sum = lax.fori_loop(0, 4, qkv_back, (zero_row, zero_row))
    ag_start(2, g3)
    vecg[64:65, :] = gain_sum
    vecg[66:67, :] = bias_sum

    ones = jnp.full((16, PAD), 1.0, BF)
    v_sum = nt(ones, totb[256:512, :])
    smx[0] = jnp.zeros((16, 128), F32)
    for k in range(5):
        smx[0, k : k + 1, :] = fc1_sum[:, 128 * k : 128 * k + 128]
    smx[0, 5:6, :] = q_sums[0]
    smx[0, 6:7, :] = q_sums[1]
    smx[0, 7:8, :] = v_sum[0:1, 0:128]
    smx[0, 8:9, :] = v_sum[0:1, 128:256]
    cp = rcopy(smx.at[0], smx.at[1], sx_s, sx_r, sib)
    cp.start()
    pending.append(cp)

    for k in range(3):
        at = slice(384 * k, 384 * k + 384)
        qkv_grad = tn(attin[:, at], gs[...])
        fulla[at, 128:256] = fulla[at, 128:256] + qkv_grad[:, 0:128]
        fulla[at, 256:512] = qkv_grad[:, 128:384]
        fulla[at, 512:640] = qkv_grad[:, 384:512] + vecg[:, at].T
    x_start(0, fulla)
    rcopy(smx.at[0], smx.at[1], sx_s, sx_r, sib).wait_recv()
    smz[z] = smx[0] + smx[1]
    for d in range(1, 4):
        cp = rcopy(smz.at[z], smz.at[z], sz_s.at[d], sz_r.at[z], zdev(zoff(d)))
        cp.start()
        pending.append(cp)
    z_start(0, fulla)
    c_start(1, fullb)

    g_in = rs_sum(3, part4, rr4)
    normed_one, inv_one = stats(tokp[own, :].astype(F32))
    scaled = g_in * gain0
    grad_tok = gao[...] + inv_one * (
        scaled - mean_rows(scaled) - normed_one * mean_rows(scaled * normed_one)
    )
    g4[own, :] = grad_tok.astype(BF)
    ag_start(3, g4)

    for d in range(1, 4):
        j = zoff(d)
        rcopy(smz.at[j], smz.at[j], sz_s.at[d], sz_r.at[j], zdev(j)).wait_recv()
    smc[0] = smz[0] + smz[1] + smz[2] + smz[3]
    cp = rcopy(smc.at[0], smc.at[1], sc_s, sc_r, octx)
    cp.start()
    pending.append(cp)
    c_start(0, fulla)
    c_finish(2, gc_ref)
    c_finish(1, gb_ref)
    ag_wait(2, g3)
    out_ref[...] = g3[0:ROWS, :]
    c_finish(0, ga_ref)
    wide = jnp.concatenate([ga_ref[:, 512:640], jnp.zeros((112, 128), F32)], axis=0)
    vt[t] = wide.T[64:72, :]
    for d in range(1, 8):
        cp = rcopy(vt.at[t], vt.at[t], v_s.at[d], v_r.at[t], {"tp": tpd(d)})
        cp.start()
        pending.append(cp)
    rcopy(smc.at[0], smc.at[1], sc_s, sc_r, octx).wait_recv()
    small_ref[...] = smc[0] + smc[1]
    ag_wait(3, g4)

    def spread(i, _):
        at = rows_at(i * 16, 16)
        gtok_ref[at, :] = g4[at, :].astype(F32)
        return 0

    lax.fori_loop(0, ROWS // 16, spread, 0)
    for d in range(1, 8):
        j = tpd(d)
        rcopy(vt.at[j], vt.at[j], v_s.at[d], v_r.at[j], {"tp": j}).wait_recv()
    total = vt[0]
    for j in range(1, 8):
        total = total + vt[j]
    vec_ref[...] = total

    for k, (part, rr) in enumerate(((part1, rr1), (part2, rr2), (part3, rr3), (part4, rr4))):
        rs_done(k, part, rr)
    for cp in pending:
        cp.wait_send()


def per_device(
    tokens, image_count, ln_gain, vec_bias, w_qkv, qv_bias, w_out, w_fc1, fc1_bias, w_fc2, cotangent
):
    slots, rows, width = tokens.shape
    lanes = LN - 4 * BLK - 6
    wa = jnp.concatenate(
        [w_out.T, w_qkv[0], w_qkv[1], w_qkv[2], ln_gain.T, vec_bias.T, jnp.zeros((BLK, lanes), BF)],
        axis=1,
    )
    wb = jnp.pad(w_fc1, ((0, 0), (0, LN - FF_OWN)))
    wc = jnp.pad(w_fc2.T, ((0, 0), (0, LN - FF_OWN)))
    zeros = jnp.zeros((BLK,), BF)
    row0 = jnp.concatenate([zeros[:16], qv_bias[0], zeros, qv_bias[1], jnp.zeros((192,), BF)])
    row1 = jnp.pad(fc1_bias, (0, LN - FF_OWN))
    bias_rows = jnp.concatenate(
        [row0[None], row1[None], jnp.zeros((6, LN), BF)], axis=0
    ).astype(F32)

    vm = pltpu.VMEM
    dma = pltpu.SemaphoreType.DMA
    scratch = [
        vm((D, LN), BF), vm((D, LN), BF), vm((D, LN), BF),
        vm((PAD, D), BF), vm((PAD, D), BF), vm((PAD, D), BF),
        vm((2, PAD, 128), BF), vm((4, PAD, 128), BF), vm((4, PAD, 128), BF),
        vm((768, 512), BF), vm((256, 256), BF),
        vm((2, PAD, 2 * PAD), F32),
        vm((PAD, 256), BF), vm((2, PAD, 128), BF),
        vm((PAD, D), BF), vm((PAD, D), BF), vm((PAD, D), BF), vm((PAD, D), BF),
        vm((8, OWN, D), BF), vm((8, OWN, D), BF), vm((8, OWN, D), BF), vm((8, OWN, D), BF),
        vm((PAD, D), BF), vm((PAD, D), BF), vm((PAD, D), BF), vm((PAD, D), BF),
        vm((PAD, LN), F32), vm((PAD, LN), BF), vm((PAD, LN), BF),
        vm((OWN, D), F32), vm((OWN, D), F32), vm((OWN, 128), F32), vm((OWN, D), F32),
        vm((128, D), F32), vm((128, D), F32),
        vm((D, LN), F32), vm((D, LN), F32), vm((D, LN), F32),
        vm((3, 4, BLK, LN), BF), vm((3, 4, BLK, LN), BF),
        vm((3, 4, BLK, LN), BF), vm((3, 4, BLK, LN), BF),
        vm((3, BLK, LN), BF), vm((3, BLK, LN), BF),
        vm((512, PAD), BF), vm((4, 80, PAD), BF), vm((4, 80, PAD), BF), vm((4, 128, PAD), F32),
        vm((PAD, 256), BF), vm((2, PAD, 2 * PAD), BF), vm((2, PAD, 2 * PAD), BF),
        vm((2, PAD, 128), BF), vm((PAD, 512), BF),
        vm((2, 16, 128), F32), vm((4, 16, 128), F32), vm((2, 16, 128), F32), vm((8, 8, 256), F32),
        dma((3, 3)), dma((3, 3)), dma((3, 4)), dma((3, 4)),
        dma((4,)), dma((4,)), dma((4,)), dma((4,)),
        dma((4, 8)), dma((4, 8)), dma((4, 8)), dma((4, 8)),
        dma((3,)), dma((3,)), dma((3, 4)), dma((3, 4)), dma((3,)), dma((3,)),
        dma, dma, dma((4,)), dma((4,)), dma, dma,
        dma((8,)), dma((8,)),
    ]
    vspec = pl.BlockSpec(memory_space=pltpu.VMEM)
    out, gtok, ga, gb, gc, vec, small = pl.pallas_call(
        layer_kernel,
        out_shape=(
            jax.ShapeDtypeStruct((rows, width), BF),
            jax.ShapeDtypeStruct((rows, width), F32),
            jax.ShapeDtypeStruct((BLK, LN), F32),
            jax.ShapeDtypeStruct((BLK, LN), F32),
            jax.ShapeDtypeStruct((BLK, LN), F32),
            jax.ShapeDtypeStruct((8, 256), F32),
            jax.ShapeDtypeStruct((16, 128), F32),
        ),
        in_specs=[pl.BlockSpec(memory_space=pltpu.SMEM)] + [vspec] * 6,
        out_specs=tuple([vspec] * 7),
        scratch_shapes=scratch,
        compiler_params=pltpu.CompilerParams(
            collective_id=0, has_side_effects=True, vmem_limit_bytes=62 * 2**20
        ),
        name="encoder_layer",
    )(
        image_count,
        tokens.reshape(rows, width),
        cotangent.reshape(rows, width),
        wa,
        wb,
        wc,
        bias_rows,
    )
    gains = vec[0:2, 0:BLK]
    biases = vec[2:6, 0:BLK]
    grad_qkv = jnp.stack([ga[:, BLK * (k + 1) : BLK * (k + 2)] for k in range(3)])
    grad_out = ga[:, 0:BLK].T
    grad_qv = jnp.stack(
        [
            jnp.concatenate([small[5, :HD], small[6, :HD]]),
            jnp.concatenate([small[7, :HD], small[8, :HD]]),
        ]
    )
    fc1_bias_total = small[0:5].reshape(LN)[:FF_OWN]
    return (
        out.reshape(slots, rows, width),
        gtok.reshape(slots, rows, width),
        gains,
        biases,
        grad_qkv,
        grad_qv,
        grad_out,
        gb[:, :FF_OWN],
        fc1_bias_total,
        gc[:, :FF_OWN].T,
    )


def solution(mesh):
    placed = (
        P("shard", "ctx", None),
        P("shard"),
        P(None, "shard"),
        P(None, "shard"),
        P(None, "shard", "tp"),
        P(None, "tp"),
        P("tp", "shard"),
        P("shard", "tp"),
        P("tp"),
        P("tp", "shard"),
        P("shard", "ctx", None),
    )
    return jax.shard_map(
        per_device,
        mesh=mesh,
        in_specs=placed,
        out_specs=(
            P("shard", "ctx", None),
            P("shard", "ctx", None),
            P(None, "shard"),
            P(None, "shard"),
            P(None, "shard", "tp"),
            P(None, "tp"),
            P("tp", "shard"),
            P("shard", "tp"),
            P("tp"),
            P("tp", "shard"),
        ),
        check_vma=False,
    )
```

time: 653 us -> 183 us (0.28)
  waiting for transfers between devices: 399 us -> 0 us
  Pallas kernels: 0 us -> 158 us
  blocking collectives: 125 us -> 0 us
  matrix products: 35.4 us -> 0 us
  local copies, waits for them, and re-layouts: 51.8 us -> 20.8 us
  other arithmetic: 22.2 us -> 2.13 us
  between operations: 17.1 us -> 1.38 us
    psum x5 -> x0, waiting for transfers between devices: 283 us -> none  [the longest x1 78.3 us: per_device(): mixed = lax.psum(attn_part, 'tp')]
    pallas_call x0 -> x1, Pallas kernels: none -> 158 us  [per_device(): pl.pallas_call(layer_kernel, out_shape=(jax.ShapeDtypeStruct((rows, width...]
    unnamed x21 -> x0, waiting for transfers between devices: 97.7 us -> none
    all_gather x6 -> x0, blocking collectives: 80.9 us -> none  [the longest x1 17.9 us: per_device(): lax.all_gather(w_qkv, 'shard', axis=1, tiled=True)]
    psum x2 -> x0, blocking collectives: 44.5 us -> none  [the longest x1 37.4 us: per_device(): lax.psum((grad_qv_bias, grad_fc1_bias), ('shard', 'ctx'))]
    unnamed x120 -> x13, local copies, waits for them, and re-layouts: 41.5 us -> 6.24 us
    dot_general x16 -> x0, matrix products: 33 us -> none  [the longest x3 9.25 us: matmul(): return jnp.dot(left, right, preferred_element_type=jnp.float32)]
    reduce_scatter x2 -> x0, waiting for transfers between devices: 18.4 us -> none  [the longest x1 18.4 us: per_device(): lax.psum_scatter(grad_fc2, 'shard', scatter_dimension=1, tiled=True)]
  transfers between devices with their start and end apart: 15 -> 0, of which waited for: 9 -> 0; matrix products, arithmetic and copies ran while one was open for 9% -> 0% of each run, Pallas kernels for 0% -> 0%
where the time goes in v1:
time: 183 us
  Pallas kernels  158 us (86%)
  local copies, waits for them, and re-layouts  20.8 us (11%)
  other arithmetic  2.13 us (1%)
    pallas_call x1, Pallas kernels, per_device(): pl.pallas_call(layer_kernel, out_shape=(jax.ShapeDtypeStruct((rows, width...  158 us
    unnamed x13, local copies, waits for them, and re-layouts  6.24 us

profile of v1, /device:TPU:0, one launch (start us, length us, event | category | flops | bytes accessed | tf_op | source)
XLA Modules:
  0.0 182.7 jit_solution(13105069341103599037)
XLA Ops:
  1.3 0.1 pad.25.clone
  1.4 0.8 slice_reduce_fusion
  2.2 0.1 concatenate.16
  2.3 0.7 pad.13
  3.0 0.7 maximum_convert_fusion.bias_rows
  3.7 0.8 copy.22
  4.5 0.8 copy.23
  5.3 1.0 copy.21
  6.3 1.6 pad.11.wb_in
  7.9 1.6 pad.12.wc_in
  9.5 1.0 slice_bitcast_fusion.5
  10.5 0.9 concatenate.15.wa_in
  11.4 158.4 %encoder_layer.1 = (bf16[368,1152]{1,0:T(8,128)(2,1)}, f32[368,1152]{1,0:T(8,128)}, f32[144,640]{1,0:T(8,128)}, f32[144,640]{1,0:T(8,128)}, f32[144,640]{1,0:T(8...) custom-call(s32[1]{0:T(128)S(6)} %copy.28.count, bf16[368,1152]{1,0:T(8,128)(2,1)} %bitcast.39, bf16[368,1152]{1,0:T(8,128)(2,1)} %bitcast.40, ...), custom_call_target="tpu_custom_call" | custom-call | tf_op jit(solution)/shard_map/encoder_layer/pallas_call | solution.py:706
  169.7 0.0 copy-start.1
  169.8 1.4 slice.62
  171.1 1.3 slice.63
  172.4 0.8 slice_bitcast_fusion.12
  173.2 1.3 slice_bitcast_fusion.8
  174.5 0.1 pad_maximum_fusion.2
  174.5 0.6 pad_maximum_fusion.1
  175.1 1.7 slice_bitcast_fusion
  176.9 1.4 slice_bitcast_fusion.1
  178.3 0.0 copy-start
  178.3 0.8 copy.24
  179.0 0.8 pad_maximum_fusion
  179.8 0.0 copy-done.1
  179.8 0.9 copy.29
  180.7 0.0 copy-done
  180.7 0.0 copy-start.2
  180.7 1.2 copy.30
  181.9 0.0 copy-done.2
  182.0 0.7 copy.31
  (7 shorter events, 0.0 us)
Async XLA Ops:
  169.7 10.1 %copy-start.1 = (bf16[368,1152]{1,0:T(8,128)(2,1)S(1)}, bf16[368,1152]{1,0:T(8,128)(2,1)}, u32[]{:S(2)}) copy-start(bf16[368,1152]{1,0:T(8,128)(2,1)} %get-tuple-element.17) | copy-start | bytes 2543620
  178.3 2.5 %copy-start = (f32[368,1152]{1,0:T(8,128)S(1)}, f32[368,1152]{1,0:T(8,128)}, u32[]{:S(2)}) copy-start(f32[368,1152]{1,0:T(8,128)} %get-tuple-element.18) | copy-start | bytes 5087236
  180.7 1.2 copy-start.2

commit v2 on v1

--- a/solution.py
+++ b/solution.py
@@ -65,17 +65,30 @@
     count,
     tok,
     cot,
+    gain_in,
+    vec_in,
+    wqkv_in,
+    qv_in,
+    wout_in,
+    fc1_in,
+    fc1b_in,
+    fc2_in,
+    out_ref,
+    gtok_ref,
+    gain_out,
+    vec_out,
+    gqkv_out,
+    gqv_out,
+    gout_out,
+    gfc1_out,
+    gfc1b_out,
+    gfc2_out,
     wa_in,
     wb_in,
     wc_in,
     bias_rows,
-    out_ref,
-    gtok_ref,
+    vecs_in,
     ga_ref,
-    gb_ref,
-    gc_ref,
-    vec_ref,
-    small_ref,
     wa,
     wb,
     wc,
@@ -177,6 +190,15 @@
     def tpd(d):
         return lax.rem(t + d, 8)
 
+    lo = t // 4
+    ty = lax.rem(t, 4)
+
+    def tpat(across, along):
+        return lax.rem(lo + across, 2) * 4 + lax.rem(ty + along + 4, 4)
+
+    def near_chunk(i):
+        return lax.rem(lo + lax.div(i, 2), 2) * 2 + lax.rem(lax.div(ty, 2) + i, 2)
+
     pending = []
 
     bar = pltpu.get_barrier_semaphore()
@@ -186,6 +208,21 @@
         pl.semaphore_signal(bar, inc=1, device_id=zdev(zoff(d)), device_id_type=MESH)
     pl.semaphore_signal(bar, inc=1, device_id=sib, device_id_type=MESH)
     pl.semaphore_signal(bar, inc=1, device_id=octx, device_id_type=MESH)
+
+    def shifted(height, offset, lanes=LN):
+        row = lax.broadcasted_iota(jnp.int32, (height, lanes), 0)
+        lane = lax.broadcasted_iota(jnp.int32, (height, lanes), 1)
+        return jnp.where(lane == row + offset, 1.0, 0.0).astype(BF)
+
+    vecs_in[...] = jnp.zeros_like(vecs_in)
+    vecs_in[0:2, :] = gain_in[...].astype(F32)
+    vecs_in[2:6, :] = vec_in[...].astype(F32)
+    packed = tn(wout_in[...], shifted(BLK, 0)) + tn(
+        vecs_in[...].astype(BF), shifted(16, 4 * BLK)
+    )
+    for k in range(3):
+        packed = packed + nn(wqkv_in[k], shifted(BLK, BLK * (k + 1)))
+    wa_in[...] = packed.astype(BF)
     pl.semaphore_wait(bar, 12)
 
     groups = ((wa_in, wa), (wb_in, wb), (wc_in, wc))
@@ -220,6 +257,16 @@
             rcopy(got, got, wc_s.at[g, d], wc_r.at[g, d], sib).wait_recv()
 
     w_start(0)
+    for held, given in ((wb_in, fc1_in), (wc_in, fc2_in)):
+        held[:, 512:LN] = jnp.zeros((BLK, LN - 512), BF)
+        held[:, 0:FF_OWN] = given[...]
+    vecs_in[8:10, :] = qv_in[...].astype(F32)
+    qv_low = vecs_in[8:16, :].astype(BF)
+    bias_rows[...] = jnp.zeros_like(bias_rows)
+    bias_rows[1:2, 0:FF_OWN] = fc1b_in[...].astype(F32)
+    bias_rows[0:1, :] = (
+        nn(qv_low, shifted(BLK, 16))[0:1, :] + nn(qv_low, shifted(BLK, 16 + 2 * BLK))[1:2, :]
+    )
 
     def rs_send(k, part, rr, j):
         @pl.when(j != t)
@@ -227,9 +274,6 @@
             rcopy(
                 part.at[rows_at(j * OWN, OWN)], rr.at[t], rs_s.at[k, j], rs_r.at[k, t], {"tp": j}
             ).start()
-
-    def rs_chunk(i):
-        return lax.rem(t // 2 + 1 + i, 4)
 
     def rs_sum(k, part, rr):
         total = part[rows_at(t * OWN, OWN), :].astype(F32)
@@ -246,24 +290,37 @@
                 part.at[rows_at(j * OWN, OWN)], rr.at[t], rs_s.at[k, j], rs_r.at[k, t], {"tp": j}
             ).wait_send()
 
+    across, opposite = tpat(1, 0), tpat(0, 2)
+
+    def ag_send(k, buf, n, owner, dest):
+        blk = buf.at[rows_at(owner * OWN, OWN)]
+        cp = rcopy(blk, blk, ag_s.at[k, n], ag_r.at[k, owner], {"tp": dest})
+        cp.start()
+        pending.append(cp)
+
+    def ag_recv(k, buf, owner):
+        blk = buf.at[rows_at(owner * OWN, OWN)]
+        rcopy(blk, blk, ag_s.at[k, 0], ag_r.at[k, owner], {"tp": across}).wait_recv()
+
     def ag_start(k, buf):
-        mine = buf.at[rows_at(t * OWN, OWN)]
-        for d in range(1, 8):
-            cp = rcopy(mine, mine, ag_s.at[k, d], ag_r.at[k, t], {"tp": tpd(d)})
-            cp.start()
-            pending.append(cp)
+        for n, dest in enumerate((across, opposite, tpat(0, 1), tpat(0, -1))):
+            ag_send(k, buf, n, t, dest)
+
+    def ag_relay(k, buf):
+        ag_recv(k, buf, across)
+        ag_send(k, buf, 4, across, tpat(0, 1))
+        ag_send(k, buf, 5, across, tpat(0, -1))
+        ag_recv(k, buf, opposite)
+        ag_send(k, buf, 6, opposite, across)
 
     def ag_wait_block(k, buf, j):
-        @pl.when(j != t)
+        @pl.when((j != t) & (j != across) & (j != opposite))
         def _():
-            blk = buf.at[rows_at(j * OWN, OWN)]
-            rcopy(blk, blk, ag_s.at[k, 0], ag_r.at[k, j], {"tp": j}).wait_recv()
+            ag_recv(k, buf, j)
 
     def ag_wait(k, buf):
-        for d in range(1, 8):
-            j = tpd(d)
-            blk = buf.at[rows_at(j * OWN, OWN)]
-            rcopy(blk, blk, ag_s.at[k, 0], ag_r.at[k, j], {"tp": j}).wait_recv()
+        for a, b in ((0, 1), (0, -1), (1, 1), (1, -1), (1, 2)):
+            ag_recv(k, buf, tpat(a, b))
 
     row_i = lax.broadcasted_iota(jnp.int32, (128, 512), 0)
     lane_i = lax.broadcasted_iota(jnp.int32, (128, 512), 1)
@@ -300,8 +357,9 @@
     vecg[...] = jnp.zeros_like(vecg)
 
     w_forward(0)
+    w_start(1)
+    w_start(2)
     w_wait(0)
-    w_start(1)
     vrows[...] = wa[:, 512:640].astype(F32).T
     gain0 = vrows[64:65, :]
     gain1 = vrows[65:66, :]
@@ -311,28 +369,23 @@
     bias3 = vrows[69:70, :]
 
     def norm_one(i, _):
-        at = rows_at(i * 48, 48)
+        at = rows_at(i * 128, 128)
         normed, _inv = stats(tokp[at, :].astype(F32))
         attin[at, :] = (normed * gain0 + bias0).astype(BF)
         return 0
 
-    lax.fori_loop(0, 8, norm_one, 0)
-
-    def project(i, _):
-        at = rows_at(i * 128, 128)
-        low = (nn(attin[at, :], wa[:, 128:640]) + bias_rows[0:1, 0:512]).astype(BF)
-        heads = nt(low, sel[...]).astype(BF)
-        for j in range(2):
-            qh[j, at, :] = heads[:, 128 * j : 128 * j + 128]
-        for j in range(4):
-            kvo[j, at, :] = heads[:, 256 + 128 * j : 384 + 128 * j]
-        return 0
-
-    lax.fori_loop(0, 3, project, 0)
-    for j in range(4):
-        cp = rcopy(kvo.at[j], kvx.at[j], kv_s.at[j], kv_r.at[j], octx)
-        cp.start()
-        pending.append(cp)
+    lax.fori_loop(0, 3, norm_one, 0)
+
+    low = (nn(attin[...], wa[:, 128:640]) + bias_rows[0:1, 0:512]).astype(BF)
+    for j in (2, 3, 4, 5, 0, 1):
+        head = nt(low, sel[128 * j : 128 * j + 128, :]).astype(BF)
+        if j < 2:
+            qh[j] = head
+        else:
+            kvo[j - 2] = head
+            cp = rcopy(kvo.at[j - 2], kvx.at[j - 2], kv_s.at[j - 2], kv_r.at[j - 2], octx)
+            cp.start()
+            pending.append(cp)
 
     lane_k = lax.broadcasted_iota(jnp.int32, (128, PAD), 1)
     own_keys = jnp.minimum(limit, ROWS)
@@ -346,14 +399,14 @@
         return 0
 
     lax.fori_loop(0, 3, own_scores, 0)
-    w_forward(1)
-    w_start(2)
-    for j in range(4):
+    def kv_wait(j):
         rcopy(kvo.at[j], kvx.at[j], kv_s.at[j], kv_r.at[j], octx).wait_recv()
 
-    def attend(i, _):
+    kv_wait(0)
+    kv_wait(1)
+
+    def softmax(i, _):
         at = rows_at(i * 128, 128)
-        lows = []
         for h in range(2):
             sc = nt(qh[h, at, :], kvx[h]) * SCALE
             sc = jnp.where(lane_k < other_keys, sc, -1e30)
@@ -370,21 +423,20 @@
             px = ex * inv
             prob[h, at, 0:PAD] = po
             prob[h, at, PAD : 2 * PAD] = px
-            pol = po.astype(BF)
-            pxl = px.astype(BF)
-            pbf[h, at, 0:PAD] = pol
-            pbf[h, at, PAD : 2 * PAD] = pxl
-            low = (nn(pol, kvo[2 + h]) + nn(pxl, kvx[2 + h])).astype(BF)
-            atth[h, at, :] = low
-            lows.append(low)
-        packed = nn(lows[0], sela[0:128, :]) + nn(lows[1], sela[128:256, :])
-        att[at, :] = packed.astype(BF)
+            pbf[h, at, 0:PAD] = po.astype(BF)
+            pbf[h, at, PAD : 2 * PAD] = px.astype(BF)
         return 0
 
-    lax.fori_loop(0, 3, attend, 0)
+    lax.fori_loop(0, 3, softmax, 0)
+    kv_wait(2)
+    kv_wait(3)
+    for h in range(2):
+        low = nn(pbf[h, :, 0:PAD], kvo[2 + h]) + nn(pbf[h, :, PAD : 2 * PAD], kvx[2 + h])
+        atth[h] = low.astype(BF)
+    att[...] = (nn(atth[0], sela[0:128, :]) + nn(atth[1], sela[128:256, :])).astype(BF)
 
     def out_proj(i, _):
-        ch = rs_chunk(i)
+        ch = near_chunk(3 - i)
         at = rows_at(ch * CH, CH)
         part1[at, :] = nt(att[at, :], wa[:, 0:256]).astype(BF)
         for b in range(2):
@@ -392,16 +444,12 @@
         return 0
 
     lax.fori_loop(0, 4, out_proj, 0)
+    w_forward(1)
+    w_forward(2)
     w_wait(1)
-    w_forward(2)
     w_wait(2)
 
-    def fc2_back(i, _):
-        at = rows_at(i * 128, 128)
-        gp0[at, :] = nn(glow[at, :], wc[...])
-        return 0
-
-    lax.fori_loop(0, 3, fc2_back, 0)
+    gp0[...] = nn(glow[...], wc[...])
 
     own = rows_at(t * OWN, OWN)
     after = tokp[own, :].astype(F32) + rs_sum(0, part1, rr1) + bias2
@@ -411,9 +459,10 @@
     r2s[...] = jnp.broadcast_to(inv_two, (OWN, 128))
     g1[own, :] = (normed_two * gain1 + bias1).astype(BF)
     ag_start(0, g1)
+    ag_relay(0, g1)
 
     def mlp(i, colsum):
-        ch = lax.rem(t // 2 + i, 4)
+        ch = near_chunk(i)
         at = rows_at(ch * CH, CH)
         for b in range(2):
             ag_wait_block(0, g1, ch * 2 + b)
@@ -434,11 +483,6 @@
 
     fc1_sum = lax.fori_loop(0, 4, mlp, jnp.zeros((1, LN), F32))
 
-    def fc2_fwd(i, _):
-        at = rows_at(i * CH, CH)
-        part3[at, :] = nt(hid[at, :], wc[...]).astype(BF)
-        return 0
-
     def grad_full(full, left, right):
         for k in range(3):
             full[384 * k : 384 * k + 384, :] = tn(left[:, 384 * k : 384 * k + 384], right[...])
@@ -471,13 +515,15 @@
         cp.start()
         pending.append(cp)
 
-    def c_finish(g, ref):
+    def c_finish(g):
         rcopy(cs.at[g], cr.at[g], c_s.at[g], c_r.at[g], octx).wait_recv()
-        ref[...] = cs[g].astype(F32) + cr[g].astype(F32)
+
+    def cr_sum(g):
+        return cs[g].astype(F32) + cr[g].astype(F32)
 
     grad_full(fullc, glow, hid)
     x_start(2, fullc)
-    lax.fori_loop(0, 4, fc2_fwd, 0)
+    part3[...] = nt(hid[...], wc[...]).astype(BF)
 
     g_mlp = rs_sum(1, part2, rr2)
     scaled = g_mlp * gain1
@@ -495,6 +541,7 @@
     vecg[69:70, :] = jnp.sum(grad_y, axis=0, keepdims=True)
 
     z_start(2, fullc)
+    ag_relay(1, g2)
     grad_full(fullb, g1, gpb)
     x_start(1, fullb)
 
@@ -503,15 +550,9 @@
         rs_send(2, part3, rr3, lax.rem(t + j, 8))
     z_start(1, fullb)
 
-    def grad_att(i, _):
-        at = rows_at(i * 128, 128)
-        low = nn(g2[at, :], wa[:, 0:256]).astype(BF)
-        heads = nt(low, sela[...]).astype(BF)
-        for h in range(2):
-            gah[h, at, :] = heads[:, 128 * h : 128 * h + 128]
-        return 0
-
-    lax.fori_loop(0, 3, grad_att, 0)
+    low = nn(g2[...], wa[:, 0:256]).astype(BF)
+    for h in range(2):
+        gah[h] = nt(low, sela[128 * h : 128 * h + 128, :]).astype(BF)
 
     q_sums = []
     for h in range(2):
@@ -542,10 +583,12 @@
             pending.append(cp)
 
     c_start(2, fullc)
+    c_start(1, fullb)
     for k in range(3):
         fulla[384 * k : 384 * k + 384, 0:256] = tn(g2[:, 384 * k : 384 * k + 384], att[...])
     lay = (aft[...] + rs_sum(2, part3, rr3) + bias3) * mask_at(t * OWN, OWN)
     g3[own, :] = lay.astype(BF)
+    ag_start(2, g3)
 
     for j in range(4):
         rcopy(dks.at[j], dkr.at[j], dk_s.at[j], dk_r.at[j], octx).wait_recv()
@@ -555,7 +598,7 @@
     gs[...] = (nn(dqb[...], sel[0:256, :]) + tn(totb[...], sel[256:768, :])).astype(BF)
 
     def qkv_back(i, acc):
-        ch = rs_chunk(i)
+        ch = near_chunk(3 - i)
         at = rows_at(ch * CH, CH)
         grad = nt(gs[at, :], wa[:, 128:640])
         part4[at, :] = grad.astype(BF)
@@ -569,7 +612,7 @@
 
     zero_row = jnp.zeros((1, D), F32)
     gain_sum, bias_sum = lax.fori_loop(0, 4, qkv_back, (zero_row, zero_row))
-    ag_start(2, g3)
+    ag_relay(2, g3)
     vecg[64:65, :] = gain_sum
     vecg[66:67, :] = bias_sum
 
@@ -600,7 +643,6 @@
         cp.start()
         pending.append(cp)
     z_start(0, fulla)
-    c_start(1, fullb)
 
     g_in = rs_sum(3, part4, rr4)
     normed_one, inv_one = stats(tokp[own, :].astype(F32))
@@ -610,7 +652,12 @@
     )
     g4[own, :] = grad_tok.astype(BF)
     ag_start(3, g4)
-
+    c_finish(2)
+    gfc2_out[...] = cr_sum(2)[:, 0:FF_OWN]
+    c_finish(1)
+    gfc1_out[...] = cr_sum(1)[:, 0:FF_OWN]
+    ag_relay(3, g4)
+    c_start(0, fulla)
     for d in range(1, 4):
         j = zoff(d)
         rcopy(smz.at[j], smz.at[j], sz_s.at[d], sz_r.at[j], zdev(j)).wait_recv()
@@ -618,20 +665,28 @@
     cp = rcopy(smc.at[0], smc.at[1], sc_s, sc_r, octx)
     cp.start()
     pending.append(cp)
-    c_start(0, fulla)
-    c_finish(2, gc_ref)
-    c_finish(1, gb_ref)
     ag_wait(2, g3)
     out_ref[...] = g3[0:ROWS, :]
-    c_finish(0, ga_ref)
+    c_finish(0)
+    ga_ref[...] = cr_sum(0)
     wide = jnp.concatenate([ga_ref[:, 512:640], jnp.zeros((112, 128), F32)], axis=0)
     vt[t] = wide.T[64:72, :]
     for d in range(1, 8):
         cp = rcopy(vt.at[t], vt.at[t], v_s.at[d], v_r.at[t], {"tp": tpd(d)})
         cp.start()
         pending.append(cp)
+    for k in range(3):
+        gqkv_out[k] = ga_ref[:, BLK * (k + 1) : BLK * (k + 2)]
+    wide = jnp.concatenate([ga_ref[:, 0:256], jnp.zeros((112, 256), F32)], axis=0)
+    gout_out[...] = wide.T[0:BLK, 0:BLK]
     rcopy(smc.at[0], smc.at[1], sc_s, sc_r, octx).wait_recv()
-    small_ref[...] = smc[0] + smc[1]
+    small = smc[0] + smc[1]
+    for k in range(4):
+        gfc1b_out[0:1, 128 * k : 128 * k + 128] = small[k : k + 1, :]
+    gfc1b_out[0:1, 512:FF_OWN] = small[4:5, 0 : FF_OWN - 512]
+    for k in range(4):
+        at = HD * (k % 2)
+        gqv_out[k // 2 : k // 2 + 1, at : at + HD] = small[5 + k : 6 + k, 0:HD]
     ag_wait(3, g4)
 
     def spread(i, _):
@@ -646,7 +701,8 @@
     total = vt[0]
     for j in range(1, 8):
         total = total + vt[j]
-    vec_ref[...] = total
+    gain_out[...] = total[0:2, 0:BLK]
+    vec_out[...] = total[2:6, 0:BLK]
 
     for k, (part, rr) in enumerate(((part1, rr1), (part2, rr2), (part3, rr3), (part4, rr4))):
         rs_done(k, part, rr)
@@ -654,27 +710,24 @@
         cp.wait_send()
 
 
+def deliver(*refs):
+    sems = refs[20]
+    copies = [pltpu.make_async_copy(refs[i], refs[10 + i], sems.at[i]) for i in range(10)]
+    for cp in copies:
+        cp.start()
+    for cp in copies:
+        cp.wait()
+
+
 def per_device(
     tokens, image_count, ln_gain, vec_bias, w_qkv, qv_bias, w_out, w_fc1, fc1_bias, w_fc2, cotangent
 ):
     slots, rows, width = tokens.shape
-    lanes = LN - 4 * BLK - 6
-    wa = jnp.concatenate(
-        [w_out.T, w_qkv[0], w_qkv[1], w_qkv[2], ln_gain.T, vec_bias.T, jnp.zeros((BLK, lanes), BF)],
-        axis=1,
-    )
-    wb = jnp.pad(w_fc1, ((0, 0), (0, LN - FF_OWN)))
-    wc = jnp.pad(w_fc2.T, ((0, 0), (0, LN - FF_OWN)))
-    zeros = jnp.zeros((BLK,), BF)
-    row0 = jnp.concatenate([zeros[:16], qv_bias[0], zeros, qv_bias[1], jnp.zeros((192,), BF)])
-    row1 = jnp.pad(fc1_bias, (0, LN - FF_OWN))
-    bias_rows = jnp.concatenate(
-        [row0[None], row1[None], jnp.zeros((6, LN), BF)], axis=0
-    ).astype(F32)
-
     vm = pltpu.VMEM
     dma = pltpu.SemaphoreType.DMA
     scratch = [
+        vm((BLK, LN), BF), vm((BLK, LN), BF), vm((BLK, LN), BF),
+        vm((8, LN), F32), vm((16, BLK), F32), vm((BLK, LN), F32),
         vm((D, LN), BF), vm((D, LN), BF), vm((D, LN), BF),
         vm((PAD, D), BF), vm((PAD, D), BF), vm((PAD, D), BF),
         vm((2, PAD, 128), BF), vm((4, PAD, 128), BF), vm((4, PAD, 128), BF),
@@ -703,19 +756,23 @@
         dma((8,)), dma((8,)),
     ]
     vspec = pl.BlockSpec(memory_space=pltpu.VMEM)
-    out, gtok, ga, gb, gc, vec, small = pl.pallas_call(
+    shapes = (
+        jax.ShapeDtypeStruct((rows, width), BF),
+        jax.ShapeDtypeStruct((rows, width), F32),
+        jax.ShapeDtypeStruct((2, BLK), F32),
+        jax.ShapeDtypeStruct((4, BLK), F32),
+        jax.ShapeDtypeStruct((3, BLK, BLK), F32),
+        jax.ShapeDtypeStruct((2, BLK), F32),
+        jax.ShapeDtypeStruct((BLK, BLK), F32),
+        jax.ShapeDtypeStruct((BLK, FF_OWN), F32),
+        jax.ShapeDtypeStruct((1, FF_OWN), F32),
+        jax.ShapeDtypeStruct((BLK, FF_OWN), F32),
+    )
+    results = pl.pallas_call(
         layer_kernel,
-        out_shape=(
-            jax.ShapeDtypeStruct((rows, width), BF),
-            jax.ShapeDtypeStruct((rows, width), F32),
-            jax.ShapeDtypeStruct((BLK, LN), F32),
-            jax.ShapeDtypeStruct((BLK, LN), F32),
-            jax.ShapeDtypeStruct((BLK, LN), F32),
-            jax.ShapeDtypeStruct((8, 256), F32),
-            jax.ShapeDtypeStruct((16, 128), F32),
-        ),
-        in_specs=[pl.BlockSpec(memory_space=pltpu.SMEM)] + [vspec] * 6,
-        out_specs=tuple([vspec] * 7),
+        out_shape=shapes,
+        in_specs=[pl.BlockSpec(memory_space=pltpu.SMEM)] + [vspec] * 10,
+        out_specs=tuple([vspec] * 10),
         scratch_shapes=scratch,
         compiler_params=pltpu.CompilerParams(
             collective_id=0, has_side_effects=True, vmem_limit_bytes=62 * 2**20
@@ -725,33 +782,35 @@
         image_count,
         tokens.reshape(rows, width),
         cotangent.reshape(rows, width),
-        wa,
-        wb,
-        wc,
-        bias_rows,
-    )
-    gains = vec[0:2, 0:BLK]
-    biases = vec[2:6, 0:BLK]
-    grad_qkv = jnp.stack([ga[:, BLK * (k + 1) : BLK * (k + 2)] for k in range(3)])
-    grad_out = ga[:, 0:BLK].T
-    grad_qv = jnp.stack(
-        [
-            jnp.concatenate([small[5, :HD], small[6, :HD]]),
-            jnp.concatenate([small[7, :HD], small[8, :HD]]),
-        ]
-    )
-    fc1_bias_total = small[0:5].reshape(LN)[:FF_OWN]
+        ln_gain,
+        vec_bias,
+        w_qkv,
+        qv_bias,
+        w_out,
+        w_fc1,
+        fc1_bias.reshape(1, FF_OWN),
+        w_fc2.T,
+    )
+    aspec = pl.BlockSpec(memory_space=pl.ANY)
+    out, gtok, gains, biases, gqkv, gqv, gout, gfc1, gfc1b, gfc2 = pl.pallas_call(
+        deliver,
+        out_shape=shapes,
+        in_specs=[aspec] * 10,
+        out_specs=tuple([vspec] * 10),
+        scratch_shapes=[pltpu.SemaphoreType.DMA((10,))],
+        name="deliver",
+    )(*results)
     return (
         out.reshape(slots, rows, width),
         gtok.reshape(slots, rows, width),
         gains,
         biases,
-        grad_qkv,
-        grad_qv,
-        grad_out,
-        gb[:, :FF_OWN],
-        fc1_bias_total,
-        gc[:, :FF_OWN].T,
+        gqkv,
+        gqv,
+        gout,
+        gfc1,
+        gfc1b.reshape(FF_OWN),
+        gfc2.T,
     )
 
 

time: 183 us -> 145 us (0.79)
  local copies, waits for them, and re-layouts: 20.8 us -> 1.26 us
  Pallas kernels: 158 us -> 140 us
    pallas_call x1 -> x2, Pallas kernels: 158 us -> 140 us  [the longest x1 136 us: per_device(): pl.pallas_call(layer_kernel, out_shape=shapes, in_specs=[pl.BlockSpec(mem...]
    unnamed x13 -> x0, local copies, waits for them, and re-layouts: 6.24 us -> none
    pad x3 -> x0, local copies, waits for them, and re-layouts: 3.92 us -> none  [the longest x1 1.62 us: per_device(): wb = jnp.pad(w_fc1, ((0, 0), (0, LN - FF_OWN)))]
    slice x3 -> x0, local copies, waits for them, and re-layouts: 3.42 us -> none  [the longest x1 1.35 us: per_device(): gains = vec[0:2, 0:BLK]]
    transpose x2 -> x0, local copies, waits for them, and re-layouts: 3.15 us -> none  [the longest x1 1.75 us: per_device(): gc[:, :FF_OWN]]
where the time goes in v2:
time: 145 us; the launch traced here: 144 us
  Pallas kernels  140 us (97%)
    pallas_call x1, Pallas kernels, per_device(): pl.pallas_call(layer_kernel, out_shape=shapes, in_specs=[pl.BlockSpec(mem...  136 us
    pallas_call x1, Pallas kernels, per_device(): pl.pallas_call(deliver, out_shape=shapes, in_specs=[aspec] * 10, out_spec...  4.06 us

profile of v2, /device:TPU:0, one launch (start us, length us, event | category | flops | bytes accessed | tf_op | source)
XLA Modules:
  0.0 144.3 jit_solution(8953752485241941400)
XLA Ops:
  1.3 1.3 reshape.40.fc1b_in
  2.6 136.4 %encoder_layer.1 = (bf16[368,1152]{1,0:T(8,128)(2,1)}, f32[368,1152]{1,0:T(8,128)}, f32[2,144]{1,0:T(2,128)}, f32[4,144]{1,0:T(4,128)}, f32[3,144,144]{2,1,0:T(8...) custom-call(s32[1]{0:T(128)S(6)} %copy.21.count, ...), custom_call_target="tpu_custom_call" | custom-call | tf_op jit(solution)/shard_map/encoder_layer/pallas_call | solution.py:771
  139.0 4.1 %deliver.1 = (bf16[368,1152]{1,0:T(8,128)(2,1)}, f32[368,1152]{1,0:T(8,128)}, f32[2,144]{1,0:T(2,128)}, f32[4,144]{1,0:T(4,128)}, f32[3,144,144]{2,1,0:T(8,128)}...) custom-call(bf16[368,1152]{1,0:T(8,128)(2,1)} %get-tuple-element.30., ...), custom_call_target="tpu_custom_call" | custom-call | tf_op jit(solution)/shard_map/deliver/pallas_call | solution.py:795
  143.0 1.3 reduce

commit v3 on v2

--- a/solution.py
+++ b/solution.py
@@ -263,7 +263,7 @@
     vecs_in[8:10, :] = qv_in[...].astype(F32)
     qv_low = vecs_in[8:16, :].astype(BF)
     bias_rows[...] = jnp.zeros_like(bias_rows)
-    bias_rows[1:2, 0:FF_OWN] = fc1b_in[...].astype(F32)
+    bias_rows[1:2, 0:FF_OWN] = fc1b_in[...].astype(F32).reshape(1, FF_OWN)
     bias_rows[0:1, :] = (
         nn(qv_low, shifted(BLK, 16))[0:1, :] + nn(qv_low, shifted(BLK, 16 + 2 * BLK))[1:2, :]
     )
@@ -521,9 +521,12 @@
     def cr_sum(g):
         return cs[g].astype(F32) + cr[g].astype(F32)
 
+    part3[...] = nt(hid[...], wc[...]).astype(BF)
+    for i in range(4):
+        for b in range(2):
+            rs_send(2, part3, rr3, near_chunk(3 - i) * 2 + b)
     grad_full(fullc, glow, hid)
     x_start(2, fullc)
-    part3[...] = nt(hid[...], wc[...]).astype(BF)
 
     g_mlp = rs_sum(1, part2, rr2)
     scaled = g_mlp * gain1
@@ -546,14 +549,15 @@
     x_start(1, fullb)
 
     ag_wait(1, g2)
-    for j in range(8):
-        rs_send(2, part3, rr3, lax.rem(t + j, 8))
-    z_start(1, fullb)
+    lay = (aft[...] + rs_sum(2, part3, rr3) + bias3) * mask_at(t * OWN, OWN)
+    g3[own, :] = lay.astype(BF)
+    ag_start(2, g3)
 
     low = nn(g2[...], wa[:, 0:256]).astype(BF)
     for h in range(2):
         gah[h] = nt(low, sela[128 * h : 128 * h + 128, :]).astype(BF)
 
+    z_start(1, fullb)
     q_sums = []
     for h in range(2):
 
@@ -582,13 +586,9 @@
             cp.start()
             pending.append(cp)
 
-    c_start(2, fullc)
-    c_start(1, fullb)
     for k in range(3):
         fulla[384 * k : 384 * k + 384, 0:256] = tn(g2[:, 384 * k : 384 * k + 384], att[...])
-    lay = (aft[...] + rs_sum(2, part3, rr3) + bias3) * mask_at(t * OWN, OWN)
-    g3[own, :] = lay.astype(BF)
-    ag_start(2, g3)
+    ag_relay(2, g3)
 
     for j in range(4):
         rcopy(dks.at[j], dkr.at[j], dk_s.at[j], dk_r.at[j], octx).wait_recv()
@@ -612,7 +612,8 @@
 
     zero_row = jnp.zeros((1, D), F32)
     gain_sum, bias_sum = lax.fori_loop(0, 4, qkv_back, (zero_row, zero_row))
-    ag_relay(2, g3)
+    c_start(2, fullc)
+    c_start(1, fullb)
     vecg[64:65, :] = gain_sum
     vecg[66:67, :] = bias_sum
 
@@ -712,11 +713,14 @@
 
 def deliver(*refs):
     sems = refs[20]
-    copies = [pltpu.make_async_copy(refs[i], refs[10 + i], sems.at[i]) for i in range(10)]
+    dests = list(refs[10:20])
+    dests[8] = refs[21]
+    copies = [pltpu.make_async_copy(refs[i], dests[i], sems.at[i]) for i in range(10)]
     for cp in copies:
         cp.start()
     for cp in copies:
         cp.wait()
+    refs[18][...] = refs[21][...].reshape(FF_OWN)
 
 
 def per_device(
@@ -788,16 +792,16 @@
         qv_bias,
         w_out,
         w_fc1,
-        fc1_bias.reshape(1, FF_OWN),
+        fc1_bias,
         w_fc2.T,
     )
     aspec = pl.BlockSpec(memory_space=pl.ANY)
     out, gtok, gains, biases, gqkv, gqv, gout, gfc1, gfc1b, gfc2 = pl.pallas_call(
         deliver,
-        out_shape=shapes,
+        out_shape=shapes[:8] + (jax.ShapeDtypeStruct((FF_OWN,), F32),) + shapes[9:],
         in_specs=[aspec] * 10,
         out_specs=tuple([vspec] * 10),
-        scratch_shapes=[pltpu.SemaphoreType.DMA((10,))],
+        scratch_shapes=[pltpu.SemaphoreType.DMA((10,)), pltpu.VMEM((1, FF_OWN), F32)],
         name="deliver",
     )(*results)
     return (
@@ -809,7 +813,7 @@
         gqv,
         gout,
         gfc1,
-        gfc1b.reshape(FF_OWN),
+        gfc1b,
         gfc2.T,
     )
 

time: 145 us -> 143 us (0.986)
  no operation moved by 1% of the time
where the time goes in v3:
time: 143 us
  Pallas kernels  141 us (99%)
  between operations  1.46 us (1%)
    pallas_call x1, Pallas kernels, per_device(): pl.pallas_call(layer_kernel, out_shape=shapes, in_specs=[pl.BlockSpec(mem...  137 us
    pallas_call x1, Pallas kernels, per_device(): pl.pallas_call(deliver, out_shape=shapes[:8] + (jax.ShapeDtypeStruct((FF_...  4.06 us

profile of v3, /device:TPU:0, one launch (start us, length us, event | category | flops | bytes accessed | tf_op | source)
XLA Modules:
  0.0 142.8 jit_solution(2784784856850711279)
XLA Ops:
  1.3 137.2 %encoder_layer.1 = (bf16[368,1152]{1,0:T(8,128)(2,1)}, f32[368,1152]{1,0:T(8,128)}, f32[2,144]{1,0:T(2,128)}, f32[4,144]{1,0:T(4,128)}, f32[3,144,144]{2,1,0:T(8...) custom-call(s32[1]{0:T(128)S(6)} %copy.21.count, ...), custom_call_target="tpu_custom_call" | custom-call | tf_op jit(solution)/shard_map/encoder_layer/pallas_call | solution.py:775
  138.5 4.1 %deliver.1 = (bf16[368,1152]{1,0:T(8,128)(2,1)}, f32[368,1152]{1,0:T(8,128)}, f32[2,144]{1,0:T(2,128)}, f32[4,144]{1,0:T(4,128)}, f32[3,144,144]{2,1,0:T(8,128)}...) custom-call(bf16[368,1152]{1,0:T(8,128)(2,1)} %get-tuple-element.30.refs_, ...), custom_call_target="tpu_custom_call" | custom-call | tf_op jit(solution)/shard_map/deliver/pallas_call | solution.py:799

commit v4 on v3

--- a/solution.py
+++ b/solution.py
@@ -268,29 +268,54 @@
         nn(qv_low, shifted(BLK, 16))[0:1, :] + nn(qv_low, shifted(BLK, 16 + 2 * BLK))[1:2, :]
     )
 
+    across, opposite = tpat(1, 0), tpat(0, 2)
+
+    def rs_copy(k, part, rr, j):
+        slot = jnp.where(j // 4 == lo, ty, 4 + ty)
+        return rcopy(
+            part.at[rows_at(j * OWN, OWN)],
+            rr.at[slot],
+            rs_s.at[k, j],
+            rs_r.at[k, slot],
+            {"tp": lo * 4 + lax.rem(j, 4)},
+        )
+
     def rs_send(k, part, rr, j):
-        @pl.when(j != t)
+        @pl.when(lax.rem(j, 4) != ty)
         def _():
-            rcopy(
-                part.at[rows_at(j * OWN, OWN)], rr.at[t], rs_s.at[k, j], rs_r.at[k, t], {"tp": j}
-            ).start()
+            rs_copy(k, part, rr, j).start()
+
+    def rs_recv(k, rr, slot):
+        rcopy(rr.at[slot], rr.at[slot], rs_s.at[k, 0], rs_r.at[k, slot], {"tp": across}).wait_recv()
+
+    def rs_cross(k, rr):
+        return rcopy(
+            rr.at[4 + ty], rr.at[ty], rs_s.at[k, across], rs_r.at[k, ty], {"tp": across}
+        )
+
+    def rs_relay(k, part, rr):
+        total = part[rows_at(across * OWN, OWN), :].astype(F32)
+        for d in range(1, 4):
+            slot = 4 + lax.rem(ty + d, 4)
+            rs_recv(k, rr, slot)
+            total = total + rr[slot].astype(F32)
+        rr[4 + ty] = total.astype(BF)
+        rs_cross(k, rr).start()
 
     def rs_sum(k, part, rr):
         total = part[rows_at(t * OWN, OWN), :].astype(F32)
-        for d in range(1, 8):
-            j = tpd(d)
-            rcopy(rr.at[j], rr.at[j], rs_s.at[k, j], rs_r.at[k, j], {"tp": j}).wait_recv()
-            total = total + rr[j].astype(F32)
+        for d in (1, 3, 2, 0):
+            slot = lax.rem(ty + d, 4)
+            rs_recv(k, rr, slot)
+            total = total + rr[slot].astype(F32)
         return total
 
     def rs_done(k, part, rr):
-        for d in range(1, 8):
-            j = tpd(d)
-            rcopy(
-                part.at[rows_at(j * OWN, OWN)], rr.at[t], rs_s.at[k, j], rs_r.at[k, t], {"tp": j}
-            ).wait_send()
-
-    across, opposite = tpat(1, 0), tpat(0, 2)
+        for d in range(1, 4):
+            for a in range(2):
+                rs_copy(k, part, rr, tpat(a, d)).wait_send()
+        rs_cross(k, rr).wait_send()
+
 
     def ag_send(k, buf, n, owner, dest):
         blk = buf.at[rows_at(owner * OWN, OWN)]
@@ -446,6 +471,7 @@
     lax.fori_loop(0, 4, out_proj, 0)
     w_forward(1)
     w_forward(2)
+    rs_relay(0, part1, rr1)
     w_wait(1)
     w_wait(2)
 
@@ -525,6 +551,7 @@
     for i in range(4):
         for b in range(2):
             rs_send(2, part3, rr3, near_chunk(3 - i) * 2 + b)
+    rs_relay(1, part2, rr2)
     grad_full(fullc, glow, hid)
     x_start(2, fullc)
 
@@ -544,11 +571,14 @@
     vecg[69:70, :] = jnp.sum(grad_y, axis=0, keepdims=True)
 
     z_start(2, fullc)
+    rs_relay(2, part3, rr3)
     ag_relay(1, g2)
     grad_full(fullb, g1, gpb)
     x_start(1, fullb)
 
+    z_start(1, fullb)
     ag_wait(1, g2)
+    c_start(2, fullc)
     lay = (aft[...] + rs_sum(2, part3, rr3) + bias3) * mask_at(t * OWN, OWN)
     g3[own, :] = lay.astype(BF)
     ag_start(2, g3)
@@ -557,7 +587,6 @@
     for h in range(2):
         gah[h] = nt(low, sela[128 * h : 128 * h + 128, :]).astype(BF)
 
-    z_start(1, fullb)
     q_sums = []
     for h in range(2):
 
@@ -595,6 +624,7 @@
         totb[128 * j : 128 * j + 80, :] = (dkown[j, 0:80, :] + dkr[j].astype(F32)).astype(BF)
         totb[128 * j + 80 : 128 * j + 128, :] = jnp.zeros((48, PAD), BF)
 
+    c_start(1, fullb)
     gs[...] = (nn(dqb[...], sel[0:256, :]) + tn(totb[...], sel[256:768, :])).astype(BF)
 
     def qkv_back(i, acc):
@@ -612,8 +642,6 @@
 
     zero_row = jnp.zeros((1, D), F32)
     gain_sum, bias_sum = lax.fori_loop(0, 4, qkv_back, (zero_row, zero_row))
-    c_start(2, fullc)
-    c_start(1, fullb)
     vecg[64:65, :] = gain_sum
     vecg[66:67, :] = bias_sum
 
@@ -637,6 +665,7 @@
         fulla[at, 256:512] = qkv_grad[:, 128:384]
         fulla[at, 512:640] = qkv_grad[:, 384:512] + vecg[:, at].T
     x_start(0, fulla)
+    rs_relay(3, part4, rr4)
     rcopy(smx.at[0], smx.at[1], sx_s, sx_r, sib).wait_recv()
     smz[z] = smx[0] + smx[1]
     for d in range(1, 4):

time: 143 us -> 139 us (0.972)
  Pallas kernels: 141 us -> 137 us
    pallas_call x1, Pallas kernels: 137 us -> 133 us  [per_device(): pl.pallas_call(layer_kernel, out_shape=shapes, in_specs=[pl.BlockSpec(mem...]
where the time goes in v4:
time: 139 us; the launch traced here: 138 us
  Pallas kernels  137 us (99%)
  between operations  1.46 us (1%)
    pallas_call x1, Pallas kernels, per_device(): pl.pallas_call(layer_kernel, out_shape=shapes, in_specs=[pl.BlockSpec(mem...  133 us
    pallas_call x1, Pallas kernels, per_device(): pl.pallas_call(deliver, out_shape=shapes[:8] + (jax.ShapeDtypeStruct((FF_...  4.06 us

profile of v4, /device:TPU:0, one launch (start us, length us, event | category | flops | bytes accessed | tf_op | source)
XLA Modules:
  0.0 138.4 jit_solution(5978783655951569408)
XLA Ops:
  1.3 132.9 %encoder_layer.1 = (bf16[368,1152]{1,0:T(8,128)(2,1)}, f32[368,1152]{1,0:T(8,128)}, f32[2,144]{1,0:T(2,128)}, f32[4,144]{1,0:T(4,128)}, f32[3,144,144]{2,1,0:T(8...) custom-call(s32[1]{0:T(128)S(6)} %copy.21.count, ...), custom_call_target="tpu_custom_call" | custom-call | tf_op jit(solution)/shard_map/encoder_layer/pallas_call | solution.py:804
  134.2 4.1 %deliver.1 = (bf16[368,1152]{1,0:T(8,128)(2,1)}, f32[368,1152]{1,0:T(8,128)}, f32[2,144]{1,0:T(2,128)}, f32[4,144]{1,0:T(4,128)}, f32[3,144,144]{2,1,0:T(8,128)}...) custom-call(bf16[368,1152]{1,0:T(8,128)(2,1)} %get-tuple-element.30.refs_, ...), custom_call_target="tpu_custom_call" | custom-call | tf_op jit(solution)/shard_map/deliver/pallas_call | solution.py:828

commit v5 on v4

--- a/solution.py
+++ b/solution.py
@@ -624,7 +624,6 @@
         totb[128 * j : 128 * j + 80, :] = (dkown[j, 0:80, :] + dkr[j].astype(F32)).astype(BF)
         totb[128 * j + 80 : 128 * j + 128, :] = jnp.zeros((48, PAD), BF)
 
-    c_start(1, fullb)
     gs[...] = (nn(dqb[...], sel[0:256, :]) + tn(totb[...], sel[256:768, :])).astype(BF)
 
     def qkv_back(i, acc):
@@ -673,6 +672,7 @@
         cp.start()
         pending.append(cp)
     z_start(0, fulla)
+    c_start(1, fullb)
 
     g_in = rs_sum(3, part4, rr4)
     normed_one, inv_one = stats(tokp[own, :].astype(F32))

time: 139 us -> 139 us (level)
  no operation moved by 1% of the time
where the time goes in v5:
time: 139 us; the launch traced here: 138 us
  Pallas kernels  137 us (99%)
  between operations  1.46 us (1%)
    pallas_call x1, Pallas kernels, per_device(): pl.pallas_call(layer_kernel, out_shape=shapes, in_specs=[pl.BlockSpec(mem...  133 us
    pallas_call x1, Pallas kernels, per_device(): pl.pallas_call(deliver, out_shape=shapes[:8] + (jax.ShapeDtypeStruct((FF_...  4.06 us

profile of v5, /device:TPU:0, one launch (start us, length us, event | category | flops | bytes accessed | tf_op | source)
XLA Modules:
  0.0 138.4 jit_solution(7893092004665153735)
XLA Ops:
  1.3 132.9 %encoder_layer.1 = (bf16[368,1152]{1,0:T(8,128)(2,1)}, f32[368,1152]{1,0:T(8,128)}, f32[2,144]{1,0:T(2,128)}, f32[4,144]{1,0:T(4,128)}, f32[3,144,144]{2,1,0:T(8...) custom-call(s32[1]{0:T(128)S(6)} %copy.21.count, ...), custom_call_target="tpu_custom_call" | custom-call | tf_op jit(solution)/shard_map/encoder_layer/pallas_call | solution.py:804
  134.2 4.1 %deliver.1 = (bf16[368,1152]{1,0:T(8,128)(2,1)}, f32[368,1152]{1,0:T(8,128)}, f32[2,144]{1,0:T(2,128)}, f32[4,144]{1,0:T(4,128)}, f32[3,144,144]{2,1,0:T(8,128)}...) custom-call(bf16[368,1152]{1,0:T(8,128)(2,1)} %get-tuple-element.30.refs_, ...), custom_call_target="tpu_custom_call" | custom-call | tf_op jit(solution)/shard_map/deliver/pallas_call | solution.py:828
